TPU v7x, 32 devices: a whole 2x2x4 slice. The times are simulated.
32 devices in a mesh: grp: 2 (over x), ep: 16 (over z, y, core).
Axes of the slice: x: 2, y: 2, z: 4, core: 2. Of those that a mesh axis runs over, the one named last changes fastest.
Arguments:
- tokens: bfloat16 [4096, 3584], P(('grp', 'ep')), parts along dimension 0, may hold values from -6 to 6
- expert_ids: int32 [4096, 8], P(('grp', 'ep')), parts along dimension 0, may hold values from 0 to 15, all different within a row
- gate_weights: float32 [4096, 8], P(('grp', 'ep')), parts along dimension 0, may hold values from 0.1 to 1
- use_copy: int32 [4096, 8], P(('grp', 'ep')), parts along dimension 0, may hold values 0 or 1
- expert_weights: bfloat16 [16, 3584, 3072], P('ep'), may hold values from -0.09375 to 0.09375
Outputs:
- mixed: bfloat16 [4096, 3584], P(('grp', 'ep')), parts along dimension 0
There are 2 independent parts, one for each index of `grp`. A program takes and returns all parts, laid end to end along the dimension named above; an argument that names none is the same for every part. Nothing has to cross between parts.
Inputs may be any that keep to these rules, and one draw needn't show every extreme that they name: `expert_ids`: each token names 8 different experts.
All inputs are finite; a program needn't handle non-finite values. No bound on the sum of `use_copy` on one device may be relied on, other than what follows from the above.
Results may differ from a plain program's by a relative error of at most 0.0059.
Values may be sent and summed in bfloat16 or wider, within the bound.
A program may use at most 192 MiB of HBM per device.

v0:
```python
import jax
import jax.numpy as jnp
from jax import lax
from jax.sharding import PartitionSpec as P


def from_partner(value, axis, distance):
    return lax.ppermute(value, axis, [(i, i ^ 1 << distance) for i in range(lax.axis_size(axis))])


def expert_rows(rows, weights):
    width = weights.shape[1] // 3
    both = jnp.dot(rows, weights[:, : 2 * width], preferred_element_type=jnp.float32)
    hidden = (jax.nn.silu(both[:, :width]) * both[:, width:]).astype(jnp.bfloat16)
    output = lax.dot_general(
        hidden,
        weights[:, 2 * width :],
        (((1,), (1,)), ((), ())),
        preferred_element_type=jnp.float32,
    )
    return output.astype(jnp.bfloat16)


def per_device(tokens, expert_ids, gate_weights, use_copy, expert_weights):
    ranks = lax.axis_size("ep")
    half = ranks // 2
    partner_bit = half.bit_length() - 1
    tok_rows, top_count = expert_ids.shape
    model_width = tokens.shape[1]
    capacity = tok_rows * top_count * 5 // (8 * ranks)
    target = jnp.bitwise_xor(expert_ids, use_copy * half).reshape(-1)
    copy_flag = use_copy.reshape(-1)
    bucket = target * 2 + copy_flag
    onehot = (bucket[:, None] == jnp.arange(2 * ranks, dtype=jnp.int32)[None, :]).astype(jnp.int32)
    before = jnp.sum((jnp.cumsum(onehot, axis=0) - onehot) * onehot, axis=1)
    kept = before < capacity
    slots = 2 * ranks * capacity
    place = jnp.where(kept, (target * capacity + before) * 2 + copy_flag, slots)
    copies = jnp.repeat(tokens, top_count, axis=0)
    outgoing = jnp.zeros((slots, model_width), jnp.bfloat16).at[place].set(copies, mode="drop")
    outgoing = outgoing.reshape(ranks, capacity, 2, model_width)
    own_weights = expert_weights[0]
    spare_weights = from_partner(own_weights, "ep", partner_bit)
    piece = lax.all_to_all(outgoing, "ep", split_axis=0, concat_axis=0, tiled=True)
    lead = piece.shape[0]
    rows_in = piece.shape[1]
    first = expert_rows(piece[:, :, 0, :].reshape(-1, model_width), own_weights)
    second = expert_rows(piece[:, :, 1, :].reshape(-1, model_width), spare_weights)
    results = jnp.stack(
        [first.reshape(lead, rows_in, model_width), second.reshape(lead, rows_in, model_width)],
        axis=2,
    )
    returned = lax.all_to_all(results, "ep", split_axis=0, concat_axis=0, tiled=True).reshape(
        slots, model_width
    )
    picked = jnp.take(returned, jnp.minimum(place, slots - 1), axis=0).reshape(
        tok_rows, top_count, model_width
    )
    weight = jnp.where(kept.reshape(tok_rows, top_count), gate_weights, jnp.float32(0.0))
    total = jnp.zeros((tok_rows, model_width), jnp.float32)
    for choice_index in range(top_count):
        total = (
            total
            + picked[:, choice_index, :].astype(jnp.float32)
            * weight[:, choice_index : choice_index + 1]
        )
    return total.astype(jnp.bfloat16)


def solution(mesh):
    placed = (
        P(("grp", "ep"), None),
        P(("grp", "ep"), None),
        P(("grp", "ep"), None),
        P(("grp", "ep"), None),
        P("ep", None, None),
    )
    return jax.shard_map(
        per_device, mesh=mesh, in_specs=placed, out_specs=P(("grp", "ep"), None), check_vma=False
    )
```

profile of v0, /device:TPU:13, one launch (start us, length us, event | category | flops | bytes accessed | tf_op | source)
XLA Modules:
  0.0 1484.5 jit_solution(9294205232946016231)
XLA Ops:
  0.0 0.8 multiply_add_fusion
  0.8 0.1 copy.49
  0.9 0.1 add.111
  1.0 0.1 add.110
  1.1 0.8 copy.56
  1.9 0.1 copy.55
  2.0 0.1 mul.157
  2.1 0.1 reshape.153
  2.2 9.0 reduce-window.6
  11.3 0.1 copy.51
  11.5 0.1 broadcast_add_fusion
  11.8 15.2 %scatter_custom_fusion = bf16[1280,3584]{1,0:T(8,128)(2,1)} fusion(s32[1024]{0:T(1024)S(1)} %bitcast.102, bf16[]{:T(256)} %constant.19.clone.1, bf16[128,3584]{1,0:T(8,128)(2,1)S(1)} %copy-done), kind=kCustom, calls=%fused_computation.11 | custom fusion | bytes 10092546 | tf_op jit(solution)/shard_map/scatter | solution.py:40
  27.0 13.6 reshape.155
  40.6 6.9 all-to-all-start
  47.5 2.2 collective-permute-start
  49.6 669.3 %all-to-all-done = bf16[16,40,2,3584]{3,2,1,0:T(2,128)(2,1)} async-done(((bf16[16,40,2,3584]{3,2,1,0:T(2,128)(2,1)}), bf16[16,40,2,3584]{3,2,1,0:T(2,128)(2,1)}, u32[]{:S(2)}, u32[]{:S(2)}) %all-to-all-start) | async-done | bytes 9175072 | tf_op jit(solution)/shard_map/all_to_all | solution.py:44
  718.9 18.8 %fusion.39 = (bf16[16,40,1,3584]{3,2,1,0:T(2,128)(2,1)}, bf16[16,40,1,3584]{3,2,1,0:T(2,128)(2,1)S(1)}) fusion(bf16[16,40,2,3584]{3,2,1,0:T(2,128)(2,1)} %all-to-all-done), kind=kLoop, calls=%fused_computation.77 | loop fusion | bytes 18350080 | tf_op jit(solution)/shard_map/slice | solution.py:47
  737.7 6.8 copy.61
  744.6 1.1 copy.62
  745.6 14.2 fusion.2
  759.9 9.7 fusion.10
  769.6 418.5 %collective-permute-done = bf16[3584,3072]{1,0:T(8,128)(2,1)} collective-permute-done((bf16[3584,3072]{1,0:T(8,128)(2,1)}, bf16[3584,3072]{1,0:T(8,128)(2,1)}, u32[]{:S(2)}, u32[]{:S(2)}) %collective-permute-start) | collective-permute-done | bytes 22020128 | tf_op jit(solution)/shard_map/ppermute | solution.py:8
  1188.1 13.3 fusion
  1201.4 9.9 fusion.13
  1211.3 8.1 pad_maximum_fusion
  1219.4 8.7 all-to-all-start.1
  1228.3 199.0 %all-to-all-done.1 = bf16[16,40,2,3584]{3,1,2,0:T(8,128)(2,1)} async-done(((bf16[16,40,2,3584]{3,1,2,0:T(8,128)(2,1)}), bf16[16,40,2,3584]{3,1,2,0:T(8,128)(2,1)}, u32[]{:S(2)}, u32[]{:S(2)}) %all-to-all-start.1) | async-done | bytes 9175072 | tf_op jit(solution)/shard_map/all_to_all | solution.py:53
  1427.3 14.1 copy.59
  1441.4 13.6 reshape.156
  1455.0 18.6 %gather_fusion = bf16[1024,3584]{1,0:T(8,128)(2,1)} fusion(bf16[1280,3584]{1,0:T(8,128)(2,1)} %reshape.156, s32[1024]{0:T(1024)S(1)} %broadcast_clamp_fusion), kind=kCustom, calls=%fused_computation | custom fusion | bytes 14684160 | tf_op jit(solution)/shard_map/jit(_take)/gather | solution.py:56
  1473.6 7.9 copy_select_fusion
  1481.5 2.6 fusion.21
  (24 shorter events, 0.5 us)
Async XLA Ops:
  0.0 11.7 copy-start
  40.6 678.3 %all-to-all-start = ((bf16[16,40,2,3584]{3,2,1,0:T(2,128)(2,1)}), bf16[16,40,2,3584]{3,2,1,0:T(2,128)(2,1)}, u32[]{:S(2)}, u32[]{:S(2)}) async-start(bf16[16,40,2,3584]{3,2,1,0:T(2,128)(2,1)} %reshape.155), calls=%async_computation | async-start | bytes 18350080 | tf_op jit(solution)/shard_map/all_to_all | solution.py:44
  47.5 1140.6 %collective-permute-start = (bf16[3584,3072]{1,0:T(8,128)(2,1)}, bf16[3584,3072]{1,0:T(8,128)(2,1)}, u32[]{:S(2)}, u32[]{:S(2)}) collective-permute-start(bf16[3584,3072]{1,0:T(8,128)(2,1)} %bitcast.103), channel_id=1, source_target_pairs={{0,8},{1,9},{2,10},{3,11},{4,12},{5,13},{6,14},{7,15},{8,0},{9,1},... | collective-permute-start | bytes 66060296 | tf_op jit(solution)/shard_map/ppermute | solution.py:8
  1219.4 8.9 copy-start.4
  1219.4 8.9 copy-start.2
  1219.4 8.9 copy-start.3
  1219.4 207.9 %all-to-all-start.1 = ((bf16[16,40,2,3584]{3,1,2,0:T(8,128)(2,1)}), bf16[16,40,2,3584]{3,1,2,0:T(8,128)(2,1)}, u32[]{:S(2)}, u32[]{:S(2)}) async-start(bf16[16,40,2,3584]{3,1,2,0:T(8,128)(2,1)} %pad_maximum_fusion), calls=%async_computation.1 | async-start | bytes 18350080 | tf_op jit(solution)/shard_map/all_to_all | solution.py:53
  1473.6 10.5 copy-start.1
where the time goes:
time: 1500 us; the launch traced here: 1480 us
  waiting for transfers between devices  1290 us (86%)
  local copies, waits for them, and re-layouts  104 us (7%)
  matrix products  47.2 us (3%)
  other arithmetic  28.6 us (2%)
  starting transfers between devices  17.7 us (1%)
    all_to_all x1, waiting for transfers between devices, per_device(): lax.all_to_all(outgoing, 'ep', split_axis=0, concat_axis=0, tiled=True)  669 us
    ppermute x1, waiting for transfers between devices, from_partner(): lax.ppermute(value, axis, [(i, i ^ 1 << distance) for i in range(lax.axis...  418 us
    all_to_all x1, waiting for transfers between devices, per_device(): lax.all_to_all(results, 'ep', split_axis=0, concat_axis=0, tiled=True)  199 us
  transfers between devices with their start and end apart: 3, of which 3 were waited for; matrix products, arithmetic and copies ran while one was open for 3% of the time, Pallas kernels for 0%

commit v1 on v0

v1 whole, which is shorter than its diff:
```python
import jax
import jax.numpy as jnp
from jax import lax
from jax.sharding import PartitionSpec as P

CHUNKS = 2


def routing(expert_ids, gate_weights, use_copy, ranks):
    half = ranks // 2
    tok_rows, top_count = expert_ids.shape
    capacity = tok_rows * top_count * 5 // (8 * ranks)
    lanes = jnp.arange(ranks, dtype=jnp.int32)
    hit = expert_ids[:, :, None] == lanes[None, None, :]
    home = jnp.sum(jnp.where(hit & (use_copy[:, :, None] == 0), 1, 0), axis=1)
    away = jnp.sum(jnp.where(hit & (use_copy[:, :, None] == 1), 1, 0), axis=1)
    counts = jnp.concatenate([home, away], axis=1).astype(jnp.bfloat16)
    rows = jnp.arange(tok_rows, dtype=jnp.int32)
    earlier = (rows[:, None] > rows[None, :]).astype(jnp.bfloat16)
    before = jnp.dot(earlier, counts, preferred_element_type=jnp.float32)
    kept = jnp.where(before < capacity, counts.astype(jnp.float32), 0.0)
    kept = kept[:, :ranks] + kept[:, ranks:]
    weight = jnp.sum(jnp.where(hit, gate_weights[:, :, None], 0.0), axis=1)
    return weight * kept


def per_device(tokens, expert_ids, gate_weights, use_copy, expert_weights):
    ranks = lax.axis_size("ep")
    tok_rows, model_width = tokens.shape
    weights = expert_weights[0]
    width = weights.shape[1] // 3
    table = routing(expert_ids, gate_weights, use_copy, ranks)
    mine = lax.all_to_all(table.T, "ep", split_axis=0, concat_axis=0, tiled=True)
    step = tok_rows // CHUNKS
    outs = []
    for index in range(CHUNKS):
        part = tokens[index * step : (index + 1) * step]
        rows = lax.all_gather(part, "ep", axis=0, tiled=True)
        both = jnp.dot(rows, weights[:, : 2 * width], preferred_element_type=jnp.float32)
        hidden = (jax.nn.silu(both[:, :width]) * both[:, width:]).astype(jnp.bfloat16)
        output = lax.dot_general(
            hidden,
            weights[:, 2 * width :],
            (((1,), (1,)), ((), ())),
            preferred_element_type=jnp.float32,
        )
        scale = mine[:, index * step : (index + 1) * step].reshape(-1, 1)
        output = (output * scale).astype(jnp.bfloat16)
        outs.append(lax.psum_scatter(output, "ep", scatter_dimension=0, tiled=True))
    return jnp.concatenate(outs, axis=0)


def solution(mesh):
    placed = (
        P(("grp", "ep"), None),
        P(("grp", "ep"), None),
        P(("grp", "ep"), None),
        P(("grp", "ep"), None),
        P("ep", None, None),
    )
    return jax.shard_map(
        per_device, mesh=mesh, in_specs=placed, out_specs=P(("grp", "ep"), None), check_vma=False
    )
```

time: 1500 us -> 348 us (0.23)
  the two profiles are of different devices: /device:TPU:13 before, /device:TPU:0 now
where the time goes in v1:
time: 348 us
  waiting for transfers between devices  247 us (71%)
  matrix products  67.4 us (19%)
  blocking collectives  13.7 us (4%)
  between operations  13.2 us (4%)
  other arithmetic  4.3 us (1%)
    reduce_scatter x2, waiting for transfers between devices, per_device(): outs.append(lax.psum_scatter(output, 'ep', scatter_dimension=0, tiled=True))  156 us
    all_gather x2, waiting for transfers between devices, per_device(): rows = lax.all_gather(part, 'ep', axis=0, tiled=True)  90.4 us
    dot_general x2, matrix products, per_device(): jnp.dot(rows, weights[:, :2 * width], preferred_element_type=jnp.float32)  40 us
    dot_general x2, matrix products, per_device(): lax.dot_general(hidden, weights[:, 2 * width:], (((1,), (1,)), ((), ())),...  27.2 us
    all_to_all x1, blocking collectives, per_device(): lax.all_to_all(table.T, 'ep', split_axis=0, concat_axis=0, tiled=True)  13.7 us
  transfers between devices with their start and end apart: 4, of which 4 were waited for; matrix products, arithmetic and copies ran while one was open for 20% of the time, Pallas kernels for 0%

profile of v1, /device:TPU:0, one launch (start us, length us, event | category | flops | bytes accessed | tf_op | source)
XLA Modules:
  0.0 347.8 jit_solution(9317169196095504280)
XLA Ops:
  6.5 0.0 all-gather.3.cloned.1.call-start
  6.5 2.1 fusion.22
  8.7 0.0 all-gather.3.cloned.1.call-update
  8.7 0.0 all-gather.5.cloned.1.call-start
  8.7 0.7 all-gather.5.cloned.1.call-update
  9.4 0.0 reduce-scatter.3.cloned.1.call-start
  9.5 0.7 broadcast_compare_fusion
  10.2 0.7 select_reduce_fusion.1
  10.9 0.1 fusion.12
  11.1 0.7 select_reduce_fusion.2
  11.8 13.7 %all_to_all.12 = f32[16,1,128]{2,1,0:T(1,128)S(1)} all-to-all(f32[16,1,128]{2,1,0:T(1,128)S(1)} %bitcast.10), channel_id=1, replica_groups=mesh['grp'=2,'ep'=16] {'ep'}, dimensions={0} | all-to-all | bytes 16384 | tf_op jit(solution)/shard_map/all_to_all | solution.py:33
  25.5 0.1 fusion.23
  25.6 0.1 mul.39
  25.6 55.0 %all-gather.3.cloned.1.call-done = bf16[1024,3584]{1,0:T(8,128)(2,1)} async-done(((bf16[64,3584]{1,0:T(8,128)(2,1)}), bf16[1024,3584]{1,0:T(8,128)(2,1)}) %all-gather.3.cloned.1.call-update) | async-done | bytes 7340048 | tf_op jit(solution)/shard_map/all_gather | solution.py:38
  80.6 20.0 %fusion.2 = f32[1024,2048]{1,0:T(8,128)S(1)} fusion(bf16[1024,3584]{1,0:T(8,128)(2,1)} %all-gather.3.cloned.1.call-done, bf16[3584,3072]{1,0:T(8,128)(2,1)} %bitcast.11), kind=kOutput, calls=%fused_computation.4 | convolution fusion | flops 15032385536 | bytes 30408704 | tf_op jit(solution)/shard_map/dot_general | solution.py:39
  100.7 13.4 %multiply_convert_fusion.1 = bf16[1024,3584]{1,0:T(8,128)(2,1)} fusion(f32[1024]{0:T(1024)S(1)} %mul.39, bf16[3584,3072]{1,0:T(8,128)(2,1)} %bitcast.12, f32[1024,2048]{1,0:T(8,128)S(1)} %fusion.2), kind=kOutput, calls=%fused_computation.1 | convolution fusion | flops 7529824256 | bytes 23072768 | tf_op jit(solution)/shard_map/dot_general | solution.py:41
  114.1 0.0 reduce-scatter.3.cloned.1.call-update
  114.1 0.0 reduce-scatter.5.cloned.1.call-start
  114.2 0.1 mul.44
  114.2 35.4 %all-gather.5.cloned.1.call-done = bf16[1024,3584]{1,0:T(8,128)(2,1)} async-done(((bf16[64,3584]{1,0:T(8,128)(2,1)}), bf16[1024,3584]{1,0:T(8,128)(2,1)}) %all-gather.5.cloned.1.call-update) | async-done | bytes 7340048 | tf_op jit(solution)/shard_map/all_gather | solution.py:38
  149.7 20.0 %fusion = f32[1024,2048]{1,0:T(8,128)S(1)} fusion(bf16[1024,3584]{1,0:T(8,128)(2,1)} %all-gather.5.cloned.1.call-done, bf16[3584,3072]{1,0:T(8,128)(2,1)} %bitcast.13), kind=kOutput, calls=%fused_computation.2 | convolution fusion | flops 15032385536 | bytes 30408704 | tf_op jit(solution)/shard_map/dot_general | solution.py:39
  169.7 13.8 %multiply_convert_fusion = bf16[1024,3584]{1,0:T(8,128)(2,1)} fusion(f32[1024]{0:T(1024)S(1)} %mul.44, bf16[3584,3072]{1,0:T(8,128)(2,1)} %bitcast.14, f32[1024,2048]{1,0:T(8,128)S(1)} %fusion), kind=kOutput, calls=%fused_computation | convolution fusion | flops 7529824256 | bytes 23072768 | tf_op jit(solution)/shard_map/dot_general | solution.py:41
  183.5 0.0 reduce-scatter.5.cloned.1.call-update
  183.5 60.3 %reduce-scatter.3.cloned.1.call-done = bf16[64,3584]{1,0:T(8,128)(2,1)} async-done(((bf16[1024,3584]{1,0:T(8,128)(2,1)}), bf16[64,3584]{1,0:T(8,128)(2,1)}) %reduce-scatter.3.cloned.1.call-update) | async-done | bytes 458768 | tf_op jit(solution)/shard_map/reduce_scatter | solution.py:49
  243.8 95.3 %reduce-scatter.5.cloned.1.call-done = bf16[64,3584]{1,0:T(8,128)(2,1)} async-done(((bf16[1024,3584]{1,0:T(8,128)(2,1)}), bf16[64,3584]{1,0:T(8,128)(2,1)}) %reduce-scatter.5.cloned.1.call-update) | async-done | bytes 458768 | tf_op jit(solution)/shard_map/reduce_scatter | solution.py:49
  339.1 2.1 pad_maximum_fusion
  (3 shorter events, 0.0 us)
Async XLA Ops:
  6.5 74.1 %all-gather.3.cloned.1.call-start = ((), (), s32[]{:S(2)}) async-start(), calls=%async_computation.3 | async-start | bytes 7798784 | tf_op jit(solution)/shard_map/all_gather | solution.py:38
  8.7 141.0 %all-gather.5.cloned.1.call-start = ((), (), s32[]{:S(2)}) async-start(), calls=%async_computation.5 | async-start | bytes 7798784 | tf_op jit(solution)/shard_map/all_gather | solution.py:38
  9.4 234.4 %reduce-scatter.3.cloned.1.call-start = ((), (), s32[]{:S(2)}) async-start(), calls=%async_computation.4 | async-start | bytes 7798784 | tf_op jit(solution)/shard_map/reduce_scatter | solution.py:49
  114.1 225.0 %reduce-scatter.5.cloned.1.call-start = ((), (), s32[]{:S(2)}) async-start(), calls=%async_computation.6 | async-start | bytes 7798784 | tf_op jit(solution)/shard_map/reduce_scatter | solution.py:49
Sparse Core Ops, SparseCore 0:
  9.6 70.9 all-gather.2
  82.9 66.6 all-gather.4
  153.6 90.1 reduce-scatter.2
  247.7 91.3 reduce-scatter.4

commit v2 on v1

--- a/solution.py
+++ b/solution.py
@@ -3,7 +3,7 @@
 from jax import lax
 from jax.sharding import PartitionSpec as P
 
-CHUNKS = 2
+CHUNKS = 4
 
 
 def routing(expert_ids, gate_weights, use_copy, ranks):
@@ -24,30 +24,65 @@
     return weight * kept
 
 
+def swap(value, bit):
+    ranks = lax.axis_size("ep")
+    return lax.ppermute(value, "ep", [(i, i ^ bit) for i in range(ranks)])
+
+
+def expert_rows(rows, weights, scale):
+    width = weights.shape[1] // 3
+    both = jnp.dot(rows, weights[:, : 2 * width], preferred_element_type=jnp.float32)
+    hidden = (jax.nn.silu(both[:, :width]) * both[:, width:]).astype(jnp.bfloat16)
+    output = lax.dot_general(
+        hidden,
+        weights[:, 2 * width :],
+        (((1,), (1,)), ((), ())),
+        preferred_element_type=jnp.float32,
+    )
+    return output * scale
+
+
 def per_device(tokens, expert_ids, gate_weights, use_copy, expert_weights):
     ranks = lax.axis_size("ep")
+    me = lax.axis_index("ep")
     tok_rows, model_width = tokens.shape
     weights = expert_weights[0]
-    width = weights.shape[1] // 3
-    table = routing(expert_ids, gate_weights, use_copy, ranks)
-    mine = lax.all_to_all(table.T, "ep", split_axis=0, concat_axis=0, tiled=True)
+    order = [1 << b for b in reversed(range(ranks.bit_length() - 1))]
+    stages = len(order)
+    table = routing(expert_ids, gate_weights, use_copy, ranks).T[None]
     step = tok_rows // CHUNKS
-    outs = []
-    for index in range(CHUNKS):
-        part = tokens[index * step : (index + 1) * step]
-        rows = lax.all_gather(part, "ep", axis=0, tiled=True)
-        both = jnp.dot(rows, weights[:, : 2 * width], preferred_element_type=jnp.float32)
-        hidden = (jax.nn.silu(both[:, :width]) * both[:, width:]).astype(jnp.bfloat16)
-        output = lax.dot_general(
-            hidden,
-            weights[:, 2 * width :],
-            (((1,), (1,)), ((), ())),
-            preferred_element_type=jnp.float32,
-        )
-        scale = mine[:, index * step : (index + 1) * step].reshape(-1, 1)
-        output = (output * scale).astype(jnp.bfloat16)
-        outs.append(lax.psum_scatter(output, "ep", scatter_dimension=0, tiled=True))
-    return jnp.concatenate(outs, axis=0)
+    state = [tokens[index * step : (index + 1) * step] for index in range(CHUNKS)]
+    for slot in range(CHUNKS + 2 * stages):
+        fresh = list(state)
+        for index in range(CHUNKS):
+            stage = slot - index
+            value = state[index]
+            if 0 <= stage < stages:
+                fresh[index] = (value, swap(value, order[stage]))
+            elif stage == stages:
+                scale = lax.dynamic_index_in_dim(table, me, axis=1, keepdims=False)
+                scale = scale[:, index * step : (index + 1) * step].reshape(-1, 1)
+                fresh[index] = expert_rows(value, weights, scale).astype(jnp.bfloat16)
+            elif stages < stage <= 2 * stages:
+                size = value.shape[0] // 2
+                other = swap(value[size:], order[2 * stages - stage])
+                fresh[index] = (value[:size], other)
+        if slot < stages:
+            table_next = (table, swap(table, order[slot]))
+        else:
+            table_next = table
+        fresh, table_next = lax.optimization_barrier((fresh, table_next))
+        for index in range(CHUNKS):
+            stage = slot - index
+            if 0 <= stage < stages:
+                fresh[index] = jnp.concatenate(fresh[index], axis=0)
+            elif stages < stage <= 2 * stages:
+                kept, other = fresh[index]
+                total = kept.astype(jnp.float32) + other.astype(jnp.float32)
+                fresh[index] = total.astype(jnp.bfloat16)
+        state = fresh
+        table = jnp.concatenate(table_next, axis=0) if slot < stages else table_next
+    return jnp.concatenate(state, axis=0)
 
 
 def solution(mesh):

time: 348 us -> 275 us (0.79)
  waiting for transfers between devices: 247 us -> 112 us
  starting transfers between devices: 0.12 us -> 47.6 us
  local copies, waits for them, and re-layouts: 2.34 us -> 19.9 us
  blocking collectives: 13.7 us -> 0 us
  matrix products: 67.4 us -> 80.6 us
  between operations: 13.2 us -> 0.52 us
  other arithmetic: 4.3 us -> 14.2 us
    reduce_scatter x2 -> x0, waiting for transfers between devices: 156 us -> none  [per_device(): outs.append(lax.psum_scatter(output, 'ep', scatter_dimension=0, tiled=True))]
    ppermute x0 -> x36, waiting for transfers between devices: none -> 112 us  [swap(): return lax.ppermute(value, 'ep', [(i, i ^ bit) for i in range(ranks)])]
    all_gather x2 -> x0, waiting for transfers between devices: 90.4 us -> none  [per_device(): rows = lax.all_gather(part, 'ep', axis=0, tiled=True)]
    ppermute x0 -> x36, starting transfers between devices: none -> 47.6 us  [swap(): return lax.ppermute(value, 'ep', [(i, i ^ bit) for i in range(ranks)])]
    all_to_all x1 -> x0, blocking collectives: 13.7 us -> none  [per_device(): lax.all_to_all(table.T, 'ep', split_axis=0, concat_axis=0, tiled=True)]
    dot_general x4 -> x8, matrix products: 67.2 us -> 80.5 us  [the longest x4 49.5 us: expert_rows(): jnp.dot(rows, weights[:, :2 * width], preferred_element_type=jnp.float32)]
    convert_element_type x0 -> x16, other arithmetic: none -> 11.1 us  [per_device(): fresh[index] = total.astype(jnp.bfloat16)]
    slice x2 -> x20, local copies, waits for them, and re-layouts: 2.21 us -> 9.99 us  [the longest x16 8.42 us: per_device(): other = swap(value[size:], order[2 * stages - stage])]
  transfers between devices with their start and end apart: 4 -> 36, of which waited for: 4 -> 17; matrix products, arithmetic and copies ran while one was open for 20% -> 36% of each run, Pallas kernels for 0% -> 0%
where the time goes in v2:
time: 275 us
  waiting for transfers between devices  112 us (41%)
  matrix products  80.6 us (29%)
  starting transfers between devices  47.6 us (17%)
  local copies, waits for them, and re-layouts  19.9 us (7%)
  other arithmetic  14.2 us (5%)
    ppermute x36, waiting for transfers between devices, swap(): return lax.ppermute(value, 'ep', [(i, i ^ bit) for i in range(ranks)])  112 us
    dot_general x4, matrix products, expert_rows(): jnp.dot(rows, weights[:, :2 * width], preferred_element_type=jnp.float32)  49.5 us
    ppermute x36, starting transfers between devices, swap(): return lax.ppermute(value, 'ep', [(i, i ^ bit) for i in range(ranks)])  47.6 us
    dot_general x4, matrix products, expert_rows(): lax.dot_general(hidden, weights[:, 2 * width:], (((1,), (1,)), ((), ())),...  31 us
    convert_element_type x16, other arithmetic, per_device(): fresh[index] = total.astype(jnp.bfloat16)  11.1 us
    slice x16, local copies, waits for them, and re-layouts, per_device(): other = swap(value[size:], order[2 * stages - stage])  8.42 us
  transfers between devices with their start and end apart: 36, of which 17 were waited for; matrix products, arithmetic and copies ran while one was open for 36% of the time, Pallas kernels for 0%

profile of v2, /device:TPU:0, one launch (start us, length us, event | category | flops | bytes accessed | tf_op | source)
XLA Modules:
  0.0 274.8 jit_solution(7847653863468141542)
XLA Ops:
  1.3 4.1 %collective-permute-start = (bf16[32,3584]{1,0:T(8,128)(2,1)S(1)}, bf16[32,3584]{1,0:T(8,128)(2,1)S(1)}, u32[]{:S(2)}, u32[]{:S(2)}) collective-permute-start(bf16[32,3584]{1,0:T(8,128)(2,1)S(1)} %get-tuple-element.96), channel_id=1, source_target_pairs={{0,8},{1,9},{2,10},{3,11},{4,12},{5,13},{6,14},{7,15},{8,0},{9,1},... | collective-permute-start | bytes 688136 | tf_op jit(solution)/shard_map/ppermute | solution.py:29
  7.8 8.5 %collective-permute-done.1 = f32[1,16,128]{2,1,0:T(8,128)S(1)} collective-permute-done((f32[1,16,128]{2,1,0:T(8,128)S(1)}, f32[1,16,128]{2,1,0:T(8,128)S(1)}, u32[]{:S(2)}, u32[]{:S(2)}) %collective-permute-start.1) | collective-permute-done | bytes 8224 | tf_op jit(solution)/shard_map/ppermute | solution.py:29
  17.1 3.4 %collective-permute-start.3 = (bf16[32,3584]{1,0:T(8,128)(2,1)S(1)}, bf16[32,3584]{1,0:T(8,128)(2,1)S(1)}, u32[]{:S(2)}, u32[]{:S(2)}) collective-permute-start(bf16[32,3584]{1,0:T(8,128)(2,1)S(1)} %get-tuple-element.105), channel_id=1, source_target_pairs={{0,8},{1,9},{2,10},{3,11},{4,12},{5,13},{6,14},{7,15},{8,0},{9,1},... | collective-permute-start | bytes 688136 | tf_op jit(solution)/shard_map/ppermute | solution.py:29
  20.6 12.8 %collective-permute-done.4 = f32[2,16,128]{2,1,0:T(8,128)S(1)} collective-permute-done((f32[2,16,128]{2,1,0:T(8,128)S(1)}, f32[2,16,128]{2,1,0:T(8,128)S(1)}, u32[]{:S(2)}, u32[]{:S(2)}) %collective-permute-start.4) | collective-permute-done | bytes 16416 | tf_op jit(solution)/shard_map/ppermute | solution.py:29
  34.9 3.2 %collective-permute-start.6 = (bf16[64,3584]{1,0:T(8,128)(2,1)S(1)}, bf16[64,3584]{1,0:T(8,128)(2,1)S(1)}, u32[]{:S(2)}, u32[]{:S(2)}) collective-permute-start(bf16[64,3584]{1,0:T(8,128)(2,1)S(1)} %constant_dynamic-update-slice_fusion.6), channel_id=1, source_target_pairs={{0,4},{1,5},{2,6},{3,7},{4,0},{5,1},{6,2},{7,3},{8,12},{9,13},{10,... | collective-permute-start | bytes 1376264 | tf_op jit(solution)/shard_map/ppermute | solution.py:29
  40.5 14.3 %collective-permute-done.8 = f32[4,16,128]{2,1,0:T(8,128)S(1)} collective-permute-done((f32[4,16,128]{2,1,0:T(8,128)S(1)}, f32[4,16,128]{2,1,0:T(8,128)S(1)}, u32[]{:S(2)}, u32[]{:S(2)}) %collective-permute-start.8) | collective-permute-done | bytes 32800 | tf_op jit(solution)/shard_map/ppermute | solution.py:29
  58.4 4.1 %collective-permute-start.11 = (bf16[64,3584]{1,0:T(8,128)(2,1)S(1)}, bf16[64,3584]{1,0:T(8,128)(2,1)S(1)}, u32[]{:S(2)}, u32[]{:S(2)}) collective-permute-start(bf16[64,3584]{1,0:T(8,128)(2,1)S(1)} %constant_dynamic-update-slice_fusion.14), channel_id=1, source_target_pairs={{0,4},{1,5},{2,6},{3,7},{4,0},{5,1},{6,2},{7,3},{8,12},{9,13},{10,... | collective-permute-start | bytes 1376264 | tf_op jit(solution)/shard_map/ppermute | solution.py:29
  65.6 12.0 %collective-permute-done.12 = bf16[32,3584]{1,0:T(8,128)(2,1)S(1)} collective-permute-done((bf16[32,3584]{1,0:T(8,128)(2,1)S(1)}, bf16[32,3584]{1,0:T(8,128)(2,1)S(1)}, u32[]{:S(2)}, u32[]{:S(2)}) %collective-permute-start.12) | collective-permute-done | bytes 229408 | tf_op jit(solution)/shard_map/ppermute | solution.py:29
  82.0 4.1 %collective-permute-start.16 = (bf16[64,3584]{1,0:T(8,128)(2,1)S(1)}, bf16[64,3584]{1,0:T(8,128)(2,1)S(1)}, u32[]{:S(2)}, u32[]{:S(2)}) collective-permute-start(bf16[64,3584]{1,0:T(8,128)(2,1)S(1)} %constant_dynamic-update-slice_fusion.24), channel_id=1, source_target_pairs={{0,4},{1,5},{2,6},{3,7},{4,0},{5,1},{6,2},{7,3},{8,12},{9,13},{10,... | collective-permute-start | bytes 1376264 | tf_op jit(solution)/shard_map/ppermute | solution.py:29
  86.1 12.1 %fusion.6 = f32[512,2048]{1,0:T(8,128)S(1)} fusion(bf16[3584,3072]{1,0:T(8,128)(2,1)} %bitcast.14, bf16[256,3584]{1,0:T(8,128)(2,1)} %collective-permute-done.9, bf16[256,3584]{1,0:T(8,128)(2,1)} %constant_dynamic-update-slice_fusion.10), kind=kOutput, calls=%fused_computation.6 | convolution fusion | flops 7523532800 | bytes 22544384 | tf_op jit(solution)/shard_map/dot_general | solution.py:34
  98.2 7.1 %multiply_convert_fusion.3 = bf16[512,3584]{1,0:T(8,128)(2,1)S(1)} fusion(bf16[3584,3072]{1,0:T(8,128)(2,1)} %bitcast.15, f32[512]{0:T(512)S(1)} %mul.71, f32[512,2048]{1,0:T(8,128)S(1)} %fusion.6), kind=kOutput, calls=%fused_computation.11 | convolution fusion | flops 3764912128 | bytes 15206400 | tf_op jit(solution)/shard_map/dot_general | solution.py:36
  111.5 11.4 %fusion.4 = f32[512,2048]{1,0:T(8,128)S(1)} fusion(bf16[3584,3072]{1,0:T(8,128)(2,1)} %bitcast.16, bf16[256,3584]{1,0:T(8,128)(2,1)S(1)} %copy-done.8, bf16[256,3584]{1,0:T(8,128)(2,1)S(1)} %copy-done.3), kind=kOutput, calls=%fused_computation.4 | convolution fusion | flops 7523532800 | bytes 22544384 | tf_op jit(solution)/shard_map/dot_general | solution.py:34
  122.9 7.1 %multiply_convert_fusion.2 = bf16[512,3584]{1,0:T(8,128)(2,1)S(1)} fusion(bf16[3584,3072]{1,0:T(8,128)(2,1)} %bitcast.17, f32[512]{0:T(512)S(1)} %mul.76, f32[512,2048]{1,0:T(8,128)S(1)} %fusion.4), kind=kOutput, calls=%fused_computation.10 | convolution fusion | flops 3764912128 | bytes 15206400 | tf_op jit(solution)/shard_map/dot_general | solution.py:36
  130.0 2.9 %collective-permute-done.19 = bf16[128,3584]{1,0:T(8,128)(2,1)S(1)} collective-permute-done((bf16[128,3584]{1,0:T(8,128)(2,1)S(1)}, bf16[128,3584]{1,0:T(8,128)(2,1)S(1)}, u32[]{:S(2)}, u32[]{:S(2)}) %collective-permute-start.19) | collective-permute-done | bytes 917536 | tf_op jit(solution)/shard_map/ppermute | solution.py:29
  132.9 1.9 add_convert_fusion.3
  140.4 12.6 %fusion.2 = f32[512,2048]{1,0:T(8,128)} fusion(bf16[3584,3072]{1,0:T(8,128)(2,1)} %bitcast.18, bf16[256,3584]{1,0:T(8,128)(2,1)S(1)} %collective-permute-done.18, bf16[256,3584]{1,0:T(8,128)(2,1)S(1)} %constant_dynamic-update-slice_fusion.26), kind=kOutput, calls=%fused_computation.2 | convolution fusion | flops 7523532800 | bytes 22544384 | tf_op jit(solution)/shard_map/dot_general | solution.py:34
  154.0 8.3 %multiply_convert_fusion.1 = bf16[512,3584]{1,0:T(8,128)(2,1)S(1)} fusion(bf16[3584,3072]{1,0:T(8,128)(2,1)} %bitcast.19, f32[512]{0:T(512)S(1)} %mul.81, f32[512,2048]{1,0:T(8,128)} %fusion.2), kind=kOutput, calls=%fused_computation.9 | convolution fusion | flops 3764912128 | bytes 15206400 | tf_op jit(solution)/shard_map/dot_general | solution.py:36
  164.6 2.8 %collective-permute-start.23 = (bf16[64,3584]{1,0:T(8,128)(2,1)}, bf16[64,3584]{1,0:T(8,128)(2,1)}, u32[]{:S(2)}, u32[]{:S(2)}) collective-permute-start(bf16[64,3584]{1,0:T(8,128)(2,1)} %get-tuple-element.211), channel_id=1, source_target_pairs={{0,4},{1,5},{2,6},{3,7},{4,0},{5,1},{6,2},{7,3},{8,12},{9,13},{10,... | collective-permute-start | bytes 1376264 | tf_op jit(solution)/shard_map/ppermute | solution.py:29
  167.4 1.9 add_convert_fusion.2
  172.4 13.5 %fusion = f32[512,2048]{1,0:T(8,128)} fusion(bf16[3584,3072]{1,0:T(8,128)(2,1)} %bitcast.20, bf16[256,3584]{1,0:T(8,128)(2,1)} %collective-permute-done.22, bf16[256,3584]{1,0:T(8,128)(2,1)} %constant_dynamic-update-slice_fusion.30), kind=kOutput, calls=%fused_computation | convolution fusion | flops 7523532800 | bytes 22544384 | tf_op jit(solution)/shard_map/dot_general | solution.py:34
  186.9 8.3 %multiply_convert_fusion = bf16[512,3584]{1,0:T(8,128)(2,1)S(1)} fusion(bf16[3584,3072]{1,0:T(8,128)(2,1)} %bitcast.21, f32[512]{0:T(512)S(1)} %mul.86, f32[512,2048]{1,0:T(8,128)} %fusion), kind=kOutput, calls=%fused_computation.8 | convolution fusion | flops 3764912128 | bytes 15206400 | tf_op jit(solution)/shard_map/dot_general | solution.py:36
  197.0 1.9 add_convert_fusion.1
  202.1 1.9 collective-permute-start.26
  204.1 8.4 %collective-permute-done.26 = bf16[32,3584]{1,0:T(8,128)(2,1)S(1)} collective-permute-done((bf16[32,3584]{1,0:T(8,128)(2,1)S(1)}, bf16[32,3584]{1,0:T(8,128)(2,1)S(1)}, u32[]{:S(2)}, u32[]{:S(2)}) %collective-permute-start.26) | collective-permute-done | bytes 229408 | tf_op jit(solution)/shard_map/ppermute | solution.py:29
  212.5 2.1 collective-permute-done.27
  214.6 7.1 %collective-permute-done.28 = bf16[128,3584]{1,0:T(8,128)(2,1)S(1)} collective-permute-done((bf16[128,3584]{1,0:T(8,128)(2,1)S(1)}, bf16[128,3584]{1,0:T(8,128)(2,1)S(1)}, u32[]{:S(2)}, u32[]{:S(2)}) %collective-permute-start.28) | collective-permute-done | bytes 917536 | tf_op jit(solution)/shard_map/ppermute | solution.py:29
  228.0 6.8 %collective-permute-done.30 = bf16[32,3584]{1,0:T(8,128)(2,1)S(1)} collective-permute-done((bf16[32,3584]{1,0:T(8,128)(2,1)S(1)}, bf16[32,3584]{1,0:T(8,128)(2,1)S(1)}, u32[]{:S(2)}, u32[]{:S(2)}) %collective-permute-start.30) | collective-permute-done | bytes 229408 | tf_op jit(solution)/shard_map/ppermute | solution.py:29
  234.8 6.4 %collective-permute-done.31 = bf16[64,3584]{1,0:T(8,128)(2,1)S(1)} collective-permute-done((bf16[64,3584]{1,0:T(8,128)(2,1)S(1)}, bf16[64,3584]{1,0:T(8,128)(2,1)S(1)}, u32[]{:S(2)}, u32[]{:S(2)}) %collective-permute-start.31) | collective-permute-done | bytes 458784 | tf_op jit(solution)/shard_map/ppermute | solution.py:29
  241.2 4.6 %collective-permute-done.32 = bf16[128,3584]{1,0:T(8,128)(2,1)S(1)} collective-permute-done((bf16[128,3584]{1,0:T(8,128)(2,1)S(1)}, bf16[128,3584]{1,0:T(8,128)(2,1)S(1)}, u32[]{:S(2)}, u32[]{:S(2)}) %collective-permute-start.32) | collective-permute-done | bytes 917536 | tf_op jit(solution)/shard_map/ppermute | solution.py:29
  249.2 8.3 %collective-permute-done.33 = bf16[32,3584]{1,0:T(8,128)(2,1)S(1)} collective-permute-done((bf16[32,3584]{1,0:T(8,128)(2,1)S(1)}, bf16[32,3584]{1,0:T(8,128)(2,1)S(1)}, u32[]{:S(2)}, u32[]{:S(2)}) %collective-permute-start.33) | collective-permute-done | bytes 229408 | tf_op jit(solution)/shard_map/ppermute | solution.py:29
  257.5 4.9 %collective-permute-done.34 = bf16[64,3584]{1,0:T(8,128)(2,1)S(1)} collective-permute-done((bf16[64,3584]{1,0:T(8,128)(2,1)S(1)}, bf16[64,3584]{1,0:T(8,128)(2,1)S(1)}, u32[]{:S(2)}, u32[]{:S(2)}) %collective-permute-start.34) | collective-permute-done | bytes 458784 | tf_op jit(solution)/shard_map/ppermute | solution.py:29
  264.4 9.4 %collective-permute-done.35 = bf16[32,3584]{1,0:T(8,128)(2,1)S(1)} collective-permute-done((bf16[32,3584]{1,0:T(8,128)(2,1)S(1)}, bf16[32,3584]{1,0:T(8,128)(2,1)S(1)}, u32[]{:S(2)}, u32[]{:S(2)}) %collective-permute-start.35) | collective-permute-done | bytes 229408 | tf_op jit(solution)/shard_map/ppermute | solution.py:29
  (150 shorter events, 55.9 us)
Async XLA Ops:
  1.3 15.0 %collective-permute-start = (bf16[32,3584]{1,0:T(8,128)(2,1)S(1)}, bf16[32,3584]{1,0:T(8,128)(2,1)S(1)}, u32[]{:S(2)}, u32[]{:S(2)}) collective-permute-start(bf16[32,3584]{1,0:T(8,128)(2,1)S(1)} %get-tuple-element.96), channel_id=1, source_target_pairs={{0,8},{1,9},{2,10},{3,11},{4,12},{5,13},{6,14},{7,15},{8,0},{9,1},... | collective-permute-start | bytes 688136 | tf_op jit(solution)/shard_map/ppermute | solution.py:29
  16.4 17.0 %collective-permute-start.2 = (bf16[64,3584]{1,0:T(8,128)(2,1)S(1)}, bf16[64,3584]{1,0:T(8,128)(2,1)S(1)}, u32[]{:S(2)}, u32[]{:S(2)}) collective-permute-start(bf16[64,3584]{1,0:T(8,128)(2,1)S(1)} %constant_dynamic-update-slice_fusion), channel_id=1, source_target_pairs={{0,4},{1,5},{2,6},{3,7},{4,0},{5,1},{6,2},{7,3},{8,12},{9,13},{10,... | collective-permute-start | bytes 1376264 | tf_op jit(solution)/shard_map/ppermute | solution.py:29
  17.1 16.3 %collective-permute-start.3 = (bf16[32,3584]{1,0:T(8,128)(2,1)S(1)}, bf16[32,3584]{1,0:T(8,128)(2,1)S(1)}, u32[]{:S(2)}, u32[]{:S(2)}) collective-permute-start(bf16[32,3584]{1,0:T(8,128)(2,1)S(1)} %get-tuple-element.105), channel_id=1, source_target_pairs={{0,8},{1,9},{2,10},{3,11},{4,12},{5,13},{6,14},{7,15},{8,0},{9,1},... | collective-permute-start | bytes 688136 | tf_op jit(solution)/shard_map/ppermute | solution.py:29
  20.5 12.9 %collective-permute-start.4 = (f32[2,16,128]{2,1,0:T(8,128)S(1)}, f32[2,16,128]{2,1,0:T(8,128)S(1)}, u32[]{:S(2)}, u32[]{:S(2)}) collective-permute-start(f32[2,16,128]{2,1,0:T(8,128)S(1)} %constant_dynamic-update-slice_fusion.2), channel_id=1, source_target_pairs={{0,4},{1,5},{2,6},{3,7},{4,0},{5,1},{6,2},{7,3},{8,12},{9,13},{10,... | collective-permute-start | bytes 49160 | tf_op jit(solution)/shard_map/ppermute | solution.py:29
  33.5 21.4 %collective-permute-start.5 = (bf16[128,3584]{1,0:T(8,128)(2,1)S(1)}, bf16[128,3584]{1,0:T(8,128)(2,1)S(1)}, u32[]{:S(2)}, u32[]{:S(2)}) collective-permute-start(bf16[128,3584]{1,0:T(8,128)(2,1)S(1)} %constant_dynamic-update-slice_fusion.4), channel_id=1, source_target_pairs={{0,2},{1,3},{2,0},{3,1},{4,6},{5,7},{6,4},{7,5},{8,10},{9,11},{10,... | collective-permute-start | bytes 2752520 | tf_op jit(solution)/shard_map/ppermute | solution.py:29
  34.9 20.0 %collective-permute-start.6 = (bf16[64,3584]{1,0:T(8,128)(2,1)S(1)}, bf16[64,3584]{1,0:T(8,128)(2,1)S(1)}, u32[]{:S(2)}, u32[]{:S(2)}) collective-permute-start(bf16[64,3584]{1,0:T(8,128)(2,1)S(1)} %constant_dynamic-update-slice_fusion.6), channel_id=1, source_target_pairs={{0,4},{1,5},{2,6},{3,7},{4,0},{5,1},{6,2},{7,3},{8,12},{9,13},{10,... | collective-permute-start | bytes 1376264 | tf_op jit(solution)/shard_map/ppermute | solution.py:29
  38.1 16.8 %collective-permute-start.7 = (bf16[32,3584]{1,0:T(8,128)(2,1)S(1)}, bf16[32,3584]{1,0:T(8,128)(2,1)S(1)}, u32[]{:S(2)}, u32[]{:S(2)}) collective-permute-start(bf16[32,3584]{1,0:T(8,128)(2,1)S(1)} %get-tuple-element.115), channel_id=1, source_target_pairs={{0,8},{1,9},{2,10},{3,11},{4,12},{5,13},{6,14},{7,15},{8,0},{9,1},... | collective-permute-start | bytes 688136 | tf_op jit(solution)/shard_map/ppermute | solution.py:29
  40.0 14.8 %collective-permute-start.8 = (f32[4,16,128]{2,1,0:T(8,128)S(1)}, f32[4,16,128]{2,1,0:T(8,128)S(1)}, u32[]{:S(2)}, u32[]{:S(2)}) collective-permute-start(f32[4,16,128]{2,1,0:T(8,128)S(1)} %constant_dynamic-update-slice_fusion.8), channel_id=1, source_target_pairs={{0,2},{1,3},{2,0},{3,1},{4,6},{5,7},{6,4},{7,5},{8,10},{9,11},{10,... | collective-permute-start | bytes 98312 | tf_op jit(solution)/shard_map/ppermute | solution.py:29
  56.9 22.9 %collective-permute-start.9 = (bf16[256,3584]{1,0:T(8,128)(2,1)}, bf16[256,3584]{1,0:T(8,128)(2,1)}, u32[]{:S(2)}, u32[]{:S(2)}) collective-permute-start(bf16[256,3584]{1,0:T(8,128)(2,1)} %constant_dynamic-update-slice_fusion.10), channel_id=1, source_target_pairs={{0,1},{1,0},{2,3},{3,2},{4,5},{5,4},{6,7},{7,6},{8,9},{9,8},{10,11... | collective-permute-start | bytes 5505032 | tf_op jit(solution)/shard_map/ppermute | solution.py:29
  57.0 22.8 %collective-permute-start.10 = (bf16[128,3584]{1,0:T(8,128)(2,1)S(1)}, bf16[128,3584]{1,0:T(8,128)(2,1)S(1)}, u32[]{:S(2)}, u32[]{:S(2)}) collective-permute-start(bf16[128,3584]{1,0:T(8,128)(2,1)S(1)} %constant_dynamic-update-slice_fusion.12), channel_id=1, source_target_pairs={{0,2},{1,3},{2,0},{3,1},{4,6},{5,7},{6,4},{7,5},{8,10},{9,11},{10,... | collective-permute-start | bytes 2752520 | tf_op jit(solution)/shard_map/ppermute | solution.py:29
  58.4 20.0 %collective-permute-start.11 = (bf16[64,3584]{1,0:T(8,128)(2,1)S(1)}, bf16[64,3584]{1,0:T(8,128)(2,1)S(1)}, u32[]{:S(2)}, u32[]{:S(2)}) collective-permute-start(bf16[64,3584]{1,0:T(8,128)(2,1)S(1)} %constant_dynamic-update-slice_fusion.14), channel_id=1, source_target_pairs={{0,4},{1,5},{2,6},{3,7},{4,0},{5,1},{6,2},{7,3},{8,12},{9,13},{10,... | collective-permute-start | bytes 1376264 | tf_op jit(solution)/shard_map/ppermute | solution.py:29
  62.5 15.1 %collective-permute-start.12 = (bf16[32,3584]{1,0:T(8,128)(2,1)S(1)}, bf16[32,3584]{1,0:T(8,128)(2,1)S(1)}, u32[]{:S(2)}, u32[]{:S(2)}) collective-permute-start(bf16[32,3584]{1,0:T(8,128)(2,1)S(1)} %get-tuple-element.128), channel_id=1, source_target_pairs={{0,8},{1,9},{2,10},{3,11},{4,12},{5,13},{6,14},{7,15},{8,0},{9,1},... | collective-permute-start | bytes 688136 | tf_op jit(solution)/shard_map/ppermute | solution.py:29
  80.5 24.9 %collective-permute-start.14 = (bf16[256,3584]{1,0:T(8,128)(2,1)S(1)}, bf16[256,3584]{1,0:T(8,128)(2,1)S(1)}, u32[]{:S(2)}, u32[]{:S(2)}) collective-permute-start(bf16[256,3584]{1,0:T(8,128)(2,1)S(1)} %constant_dynamic-update-slice_fusion.20), channel_id=1, source_target_pairs={{0,1},{1,0},{2,3},{3,2},{4,5},{5,4},{6,7},{7,6},{8,9},{9,8},{10,11... | collective-permute-start | bytes 5505032 | tf_op jit(solution)/shard_map/ppermute | solution.py:29
  80.6 24.8 %collective-permute-start.15 = (bf16[128,3584]{1,0:T(8,128)(2,1)S(1)}, bf16[128,3584]{1,0:T(8,128)(2,1)S(1)}, u32[]{:S(2)}, u32[]{:S(2)}) collective-permute-start(bf16[128,3584]{1,0:T(8,128)(2,1)S(1)} %constant_dynamic-update-slice_fusion.22), channel_id=1, source_target_pairs={{0,2},{1,3},{2,0},{3,1},{4,6},{5,7},{6,4},{7,5},{8,10},{9,11},{10,... | collective-permute-start | bytes 2752520 | tf_op jit(solution)/shard_map/ppermute | solution.py:29
  82.0 23.4 %collective-permute-start.16 = (bf16[64,3584]{1,0:T(8,128)(2,1)S(1)}, bf16[64,3584]{1,0:T(8,128)(2,1)S(1)}, u32[]{:S(2)}, u32[]{:S(2)}) collective-permute-start(bf16[64,3584]{1,0:T(8,128)(2,1)S(1)} %constant_dynamic-update-slice_fusion.24), channel_id=1, source_target_pairs={{0,4},{1,5},{2,6},{3,7},{4,0},{5,1},{6,2},{7,3},{8,12},{9,13},{10,... | collective-permute-start | bytes 1376264 | tf_op jit(solution)/shard_map/ppermute | solution.py:29
  107.6 25.3 %collective-permute-start.17 = (bf16[256,3584]{1,0:T(8,128)(2,1)}, bf16[256,3584]{1,0:T(8,128)(2,1)}, u32[]{:S(2)}, u32[]{:S(2)}) collective-permute-start(bf16[256,3584]{1,0:T(8,128)(2,1)} %get-tuple-element.195), channel_id=1, source_target_pairs={{0,1},{1,0},{2,3},{3,2},{4,5},{5,4},{6,7},{7,6},{8,9},{9,8},{10,11... | collective-permute-start | bytes 5505032 | tf_op jit(solution)/shard_map/ppermute | solution.py:29
  109.9 23.0 %collective-permute-start.18 = (bf16[256,3584]{1,0:T(8,128)(2,1)S(1)}, bf16[256,3584]{1,0:T(8,128)(2,1)S(1)}, u32[]{:S(2)}, u32[]{:S(2)}) collective-permute-start(bf16[256,3584]{1,0:T(8,128)(2,1)S(1)} %constant_dynamic-update-slice_fusion.26), channel_id=1, source_target_pairs={{0,1},{1,0},{2,3},{3,2},{4,5},{5,4},{6,7},{7,6},{8,9},{9,8},{10,11... | collective-permute-start | bytes 5505032 | tf_op jit(solution)/shard_map/ppermute | solution.py:29
  110.6 22.3 %collective-permute-start.19 = (bf16[128,3584]{1,0:T(8,128)(2,1)S(1)}, bf16[128,3584]{1,0:T(8,128)(2,1)S(1)}, u32[]{:S(2)}, u32[]{:S(2)}) collective-permute-start(bf16[128,3584]{1,0:T(8,128)(2,1)S(1)} %constant_dynamic-update-slice_fusion.28), channel_id=1, source_target_pairs={{0,2},{1,3},{2,0},{3,1},{4,6},{5,7},{6,4},{7,5},{8,10},{9,11},{10,... | collective-permute-start | bytes 2752520 | tf_op jit(solution)/shard_map/ppermute | solution.py:29
  135.9 26.5 %collective-permute-start.20 = (bf16[128,3584]{1,0:T(8,128)(2,1)}, bf16[128,3584]{1,0:T(8,128)(2,1)}, u32[]{:S(2)}, u32[]{:S(2)}) collective-permute-start(bf16[128,3584]{1,0:T(8,128)(2,1)} %get-tuple-element.203), channel_id=1, source_target_pairs={{0,2},{1,3},{2,0},{3,1},{4,6},{5,7},{6,4},{7,5},{8,10},{9,11},{10,... | collective-permute-start | bytes 2752520 | tf_op jit(solution)/shard_map/ppermute | solution.py:29
  137.9 24.5 %collective-permute-start.21 = (bf16[256,3584]{1,0:T(8,128)(2,1)}, bf16[256,3584]{1,0:T(8,128)(2,1)}, u32[]{:S(2)}, u32[]{:S(2)}) collective-permute-start(bf16[256,3584]{1,0:T(8,128)(2,1)} %get-tuple-element.193), channel_id=1, source_target_pairs={{0,1},{1,0},{2,3},{3,2},{4,5},{5,4},{6,7},{7,6},{8,9},{9,8},{10,11... | collective-permute-start | bytes 5505032 | tf_op jit(solution)/shard_map/ppermute | solution.py:29
  139.9 22.5 %collective-permute-start.22 = (bf16[256,3584]{1,0:T(8,128)(2,1)}, bf16[256,3584]{1,0:T(8,128)(2,1)}, u32[]{:S(2)}, u32[]{:S(2)}) collective-permute-start(bf16[256,3584]{1,0:T(8,128)(2,1)} %constant_dynamic-update-slice_fusion.30), channel_id=1, source_target_pairs={{0,1},{1,0},{2,3},{3,2},{4,5},{5,4},{6,7},{7,6},{8,9},{9,8},{10,11... | collective-permute-start | bytes 5505032 | tf_op jit(solution)/shard_map/ppermute | solution.py:29
  164.6 30.6 %collective-permute-start.23 = (bf16[64,3584]{1,0:T(8,128)(2,1)}, bf16[64,3584]{1,0:T(8,128)(2,1)}, u32[]{:S(2)}, u32[]{:S(2)}) collective-permute-start(bf16[64,3584]{1,0:T(8,128)(2,1)} %get-tuple-element.211), channel_id=1, source_target_pairs={{0,4},{1,5},{2,6},{3,7},{4,0},{5,1},{6,2},{7,3},{8,12},{9,13},{10,... | collective-permute-start | bytes 1376264 | tf_op jit(solution)/shard_map/ppermute | solution.py:29
  170.4 24.8 %collective-permute-start.24 = (bf16[128,3584]{1,0:T(8,128)(2,1)}, bf16[128,3584]{1,0:T(8,128)(2,1)}, u32[]{:S(2)}, u32[]{:S(2)}) collective-permute-start(bf16[128,3584]{1,0:T(8,128)(2,1)} %get-tuple-element.201), channel_id=1, source_target_pairs={{0,2},{1,3},{2,0},{3,1},{4,6},{5,7},{6,4},{7,5},{8,10},{9,11},{10,... | collective-permute-start | bytes 2752520 | tf_op jit(solution)/shard_map/ppermute | solution.py:29
  172.4 22.8 %collective-permute-start.25 = (bf16[256,3584]{1,0:T(8,128)(2,1)}, bf16[256,3584]{1,0:T(8,128)(2,1)}, u32[]{:S(2)}, u32[]{:S(2)}) collective-permute-start(bf16[256,3584]{1,0:T(8,128)(2,1)} %get-tuple-element.191), channel_id=1, source_target_pairs={{0,1},{1,0},{2,3},{3,2},{4,5},{5,4},{6,7},{7,6},{8,9},{9,8},{10,11... | collective-permute-start | bytes 5505032 | tf_op jit(solution)/shard_map/ppermute | solution.py:29
  196.7 17.9 %collective-permute-start.27 = (bf16[64,3584]{1,0:T(8,128)(2,1)S(1)}, bf16[64,3584]{1,0:T(8,128)(2,1)S(1)}, u32[]{:S(2)}, u32[]{:S(2)}) collective-permute-start(bf16[64,3584]{1,0:T(8,128)(2,1)S(1)} %get-tuple-element.209), channel_id=1, source_target_pairs={{0,4},{1,5},{2,6},{3,7},{4,0},{5,1},{6,2},{7,3},{8,12},{9,13},{10,... | collective-permute-start | bytes 1376264 | tf_op jit(solution)/shard_map/ppermute | solution.py:29
  199.1 22.6 %collective-permute-start.28 = (bf16[128,3584]{1,0:T(8,128)(2,1)S(1)}, bf16[128,3584]{1,0:T(8,128)(2,1)S(1)}, u32[]{:S(2)}, u32[]{:S(2)}) collective-permute-start(bf16[128,3584]{1,0:T(8,128)(2,1)S(1)} %get-tuple-element.199), channel_id=1, source_target_pairs={{0,2},{1,3},{2,0},{3,1},{4,6},{5,7},{6,4},{7,5},{8,10},{9,11},{10,... | collective-permute-start | bytes 2752520 | tf_op jit(solution)/shard_map/ppermute | solution.py:29
  200.7 21.0 %collective-permute-start.29 = (bf16[256,3584]{1,0:T(8,128)(2,1)S(1)}, bf16[256,3584]{1,0:T(8,128)(2,1)S(1)}, u32[]{:S(2)}, u32[]{:S(2)}) collective-permute-start(bf16[256,3584]{1,0:T(8,128)(2,1)S(1)} %get-tuple-element.189), channel_id=1, source_target_pairs={{0,1},{1,0},{2,3},{3,2},{4,5},{5,4},{6,7},{7,6},{8,9},{9,8},{10,11... | collective-permute-start | bytes 5505032 | tf_op jit(solution)/shard_map/ppermute | solution.py:29
  221.8 12.9 %collective-permute-start.30 = (bf16[32,3584]{1,0:T(8,128)(2,1)S(1)}, bf16[32,3584]{1,0:T(8,128)(2,1)S(1)}, u32[]{:S(2)}, u32[]{:S(2)}) collective-permute-start(bf16[32,3584]{1,0:T(8,128)(2,1)S(1)} %get-tuple-element.221), channel_id=1, source_target_pairs={{0,8},{1,9},{2,10},{3,11},{4,12},{5,13},{6,14},{7,15},{8,0},{9,1},... | collective-permute-start | bytes 688136 | tf_op jit(solution)/shard_map/ppermute | solution.py:29
  224.3 21.5 %collective-permute-start.32 = (bf16[128,3584]{1,0:T(8,128)(2,1)S(1)}, bf16[128,3584]{1,0:T(8,128)(2,1)S(1)}, u32[]{:S(2)}, u32[]{:S(2)}) collective-permute-start(bf16[128,3584]{1,0:T(8,128)(2,1)S(1)} %get-tuple-element.197), channel_id=1, source_target_pairs={{0,2},{1,3},{2,0},{3,1},{4,6},{5,7},{6,4},{7,5},{8,10},{9,11},{10,... | collective-permute-start | bytes 2752520 | tf_op jit(solution)/shard_map/ppermute | solution.py:29
  226.1 15.0 %collective-permute-start.31 = (bf16[64,3584]{1,0:T(8,128)(2,1)S(1)}, bf16[64,3584]{1,0:T(8,128)(2,1)S(1)}, u32[]{:S(2)}, u32[]{:S(2)}) collective-permute-start(bf16[64,3584]{1,0:T(8,128)(2,1)S(1)} %get-tuple-element.207), channel_id=1, source_target_pairs={{0,4},{1,5},{2,6},{3,7},{4,0},{5,1},{6,2},{7,3},{8,12},{9,13},{10,... | collective-permute-start | bytes 1376264 | tf_op jit(solution)/shard_map/ppermute | solution.py:29
  245.9 11.7 %collective-permute-start.33 = (bf16[32,3584]{1,0:T(8,128)(2,1)S(1)}, bf16[32,3584]{1,0:T(8,128)(2,1)S(1)}, u32[]{:S(2)}, u32[]{:S(2)}) collective-permute-start(bf16[32,3584]{1,0:T(8,128)(2,1)S(1)} %get-tuple-element.219), channel_id=1, source_target_pairs={{0,8},{1,9},{2,10},{3,11},{4,12},{5,13},{6,14},{7,15},{8,0},{9,1},... | collective-permute-start | bytes 688136 | tf_op jit(solution)/shard_map/ppermute | solution.py:29
  247.4 14.9 %collective-permute-start.34 = (bf16[64,3584]{1,0:T(8,128)(2,1)S(1)}, bf16[64,3584]{1,0:T(8,128)(2,1)S(1)}, u32[]{:S(2)}, u32[]{:S(2)}) collective-permute-start(bf16[64,3584]{1,0:T(8,128)(2,1)S(1)} %get-tuple-element.205), channel_id=1, source_target_pairs={{0,4},{1,5},{2,6},{3,7},{4,0},{5,1},{6,2},{7,3},{8,12},{9,13},{10,... | collective-permute-start | bytes 1376264 | tf_op jit(solution)/shard_map/ppermute | solution.py:29
  (13 other events, 62.8 us)

commit v3 on v2

--- a/solution.py
+++ b/solution.py
@@ -47,12 +47,43 @@
     me = lax.axis_index("ep")
     tok_rows, model_width = tokens.shape
     weights = expert_weights[0]
-    order = [1 << b for b in reversed(range(ranks.bit_length() - 1))]
+    order = [1 << b for b in reversed(range(1, ranks.bit_length() - 1))]
+    back = [order[-2], order[-1]] + order[:-2][::-1]
     stages = len(order)
     table = routing(expert_ids, gate_weights, use_copy, ranks).T[None]
     step = tok_rows // CHUNKS
     state = [tokens[index * step : (index + 1) * step] for index in range(CHUNKS)]
+
+    def join(pair):
+        return jnp.concatenate(pair, axis=0)
+
+    def add(pair):
+        kept, other = pair
+        return (kept.astype(jnp.float32) + other.astype(jnp.float32)).astype(jnp.bfloat16)
+
+    def halves(value, bit):
+        size = value.shape[0] // 2
+        return (value[:size], swap(value[size:], bit))
+
     for slot in range(CHUNKS + 2 * stages):
+        into, out = slot - stages, slot - stages - 1
+        opens = False
+        if 0 <= into < CHUNKS:
+            state[into] = (state[into], swap(state[into], 1))
+            opens = True
+        if 0 <= out < CHUNKS:
+            state[out] = halves(state[out], 1)
+            opens = True
+        if slot == stages:
+            table = (table, swap(table, 1))
+        if opens:
+            state, table = lax.optimization_barrier((state, table))
+        if 0 <= into < CHUNKS:
+            state[into] = join(state[into])
+        if 0 <= out < CHUNKS:
+            state[out] = add(state[out])
+        if slot == stages:
+            table = lax.dynamic_index_in_dim(join(table), me, axis=1, keepdims=False)
         fresh = list(state)
         for index in range(CHUNKS):
             stage = slot - index
@@ -60,28 +91,30 @@
             if 0 <= stage < stages:
                 fresh[index] = (value, swap(value, order[stage]))
             elif stage == stages:
-                scale = lax.dynamic_index_in_dim(table, me, axis=1, keepdims=False)
-                scale = scale[:, index * step : (index + 1) * step].reshape(-1, 1)
+                scale = table[:, index * step : (index + 1) * step].reshape(-1, 1)
                 fresh[index] = expert_rows(value, weights, scale).astype(jnp.bfloat16)
             elif stages < stage <= 2 * stages:
-                size = value.shape[0] // 2
-                other = swap(value[size:], order[2 * stages - stage])
-                fresh[index] = (value[:size], other)
+                bit = back[stage - stages - 1]
+                if stage == stages + 1:
+                    quarters = value.reshape(2, 2, -1, model_width)
+                    rows = value.shape[0] // 2
+                    sent = quarters[:, 1].reshape(rows, model_width)
+                    kept = quarters[:, 0].reshape(rows, model_width)
+                    fresh[index] = (kept, swap(sent, bit))
+                else:
+                    fresh[index] = halves(value, bit)
         if slot < stages:
-            table_next = (table, swap(table, order[slot]))
-        else:
-            table_next = table
-        fresh, table_next = lax.optimization_barrier((fresh, table_next))
+            table = (table, swap(table, order[slot]))
+        fresh, table = lax.optimization_barrier((fresh, table))
         for index in range(CHUNKS):
             stage = slot - index
             if 0 <= stage < stages:
-                fresh[index] = jnp.concatenate(fresh[index], axis=0)
+                fresh[index] = join(fresh[index])
             elif stages < stage <= 2 * stages:
-                kept, other = fresh[index]
-                total = kept.astype(jnp.float32) + other.astype(jnp.float32)
-                fresh[index] = total.astype(jnp.bfloat16)
-        state = fresh
-        table = jnp.concatenate(table_next, axis=0) if slot < stages else table_next
+                fresh[index] = add(fresh[index])
+        if slot < stages:
+            table = join(table)
+        state = list(fresh)
     return jnp.concatenate(state, axis=0)
 
 

time: 275 us -> 265 us (0.964)
  waiting for transfers between devices: 112 us -> 124 us
  local copies, waits for them, and re-layouts: 19.9 us -> 9.88 us
  starting transfers between devices: 47.6 us -> 40.7 us
  matrix products: 80.6 us -> 77.6 us
    ppermute x36, waiting for transfers between devices: 112 us -> 124 us  [swap(): return lax.ppermute(value, 'ep', [(i, i ^ bit) for i in range(ranks)])]
    ppermute x36, starting transfers between devices: 47.6 us -> 40.7 us  [swap(): return lax.ppermute(value, 'ep', [(i, i ^ bit) for i in range(ranks)])]
    slice x19, local copies, waits for them, and re-layouts: 8.65 us -> 4.43 us  [the longest x12 3.69 us: halves(): return (value[:size], swap(value[size:], bit))]
  transfers between devices with their start and end apart: 36 -> 36, of which waited for: 17 -> 21; matrix products, arithmetic and copies ran while one was open for 36% -> 34% of each run, Pallas kernels for 0% -> 0%
where the time goes in v3:
time: 265 us
  waiting for transfers between devices  124 us (47%)
  matrix products  77.6 us (29%)
  starting transfers between devices  40.7 us (15%)
  other arithmetic  12.2 us (5%)
  local copies, waits for them, and re-layouts  9.88 us (4%)
    ppermute x36, waiting for transfers between devices, swap(): return lax.ppermute(value, 'ep', [(i, i ^ bit) for i in range(ranks)])  124 us
    dot_general x4, matrix products, expert_rows(): jnp.dot(rows, weights[:, :2 * width], preferred_element_type=jnp.float32)  48.9 us
    ppermute x36, starting transfers between devices, swap(): return lax.ppermute(value, 'ep', [(i, i ^ bit) for i in range(ranks)])  40.7 us
    dot_general x4, matrix products, expert_rows(): lax.dot_general(hidden, weights[:, 2 * width:], (((1,), (1,)), ((), ())),...  28.5 us
    convert_element_type x16, other arithmetic, add(): (kept.astype(jnp.float32) + other.astype(jnp.float32)).astype(jnp.bfloat16)  8.82 us
  transfers between devices with their start and end apart: 36, of which 21 were waited for; matrix products, arithmetic and copies ran while one was open for 34% of the time, Pallas kernels for 0%

profile of v3, /device:TPU:0, one launch (start us, length us, event | category | flops | bytes accessed | tf_op | source)
XLA Modules:
  0.0 264.8 jit_solution(17252966384249963451)
XLA Ops:
  1.3 4.1 %collective-permute-start = (bf16[32,3584]{1,0:T(8,128)(2,1)S(1)}, bf16[32,3584]{1,0:T(8,128)(2,1)S(1)}, u32[]{:S(2)}, u32[]{:S(2)}) collective-permute-start(bf16[32,3584]{1,0:T(8,128)(2,1)S(1)} %get-tuple-element.111), channel_id=1, source_target_pairs={{0,8},{1,9},{2,10},{3,11},{4,12},{5,13},{6,14},{7,15},{8,0},{9,1},... | collective-permute-start | bytes 688136 | tf_op jit(solution)/shard_map/ppermute | solution.py:29
  7.8 8.5 %collective-permute-done.1 = f32[1,16,128]{2,1,0:T(8,128)S(1)} collective-permute-done((f32[1,16,128]{2,1,0:T(8,128)S(1)}, f32[1,16,128]{2,1,0:T(8,128)S(1)}, u32[]{:S(2)}, u32[]{:S(2)}) %collective-permute-start.1) | collective-permute-done | bytes 8224 | tf_op jit(solution)/shard_map/ppermute | solution.py:29
  17.1 3.4 %collective-permute-start.3 = (bf16[32,3584]{1,0:T(8,128)(2,1)S(1)}, bf16[32,3584]{1,0:T(8,128)(2,1)S(1)}, u32[]{:S(2)}, u32[]{:S(2)}) collective-permute-start(bf16[32,3584]{1,0:T(8,128)(2,1)S(1)} %get-tuple-element.120), channel_id=1, source_target_pairs={{0,8},{1,9},{2,10},{3,11},{4,12},{5,13},{6,14},{7,15},{8,0},{9,1},... | collective-permute-start | bytes 688136 | tf_op jit(solution)/shard_map/ppermute | solution.py:29
  20.6 12.8 %collective-permute-done.4 = f32[2,16,128]{2,1,0:T(8,128)S(1)} collective-permute-done((f32[2,16,128]{2,1,0:T(8,128)S(1)}, f32[2,16,128]{2,1,0:T(8,128)S(1)}, u32[]{:S(2)}, u32[]{:S(2)}) %collective-permute-start.4) | collective-permute-done | bytes 16416 | tf_op jit(solution)/shard_map/ppermute | solution.py:29
  34.9 3.2 %collective-permute-start.6 = (bf16[64,3584]{1,0:T(8,128)(2,1)S(1)}, bf16[64,3584]{1,0:T(8,128)(2,1)S(1)}, u32[]{:S(2)}, u32[]{:S(2)}) collective-permute-start(bf16[64,3584]{1,0:T(8,128)(2,1)S(1)} %constant_dynamic-update-slice_fusion.6), channel_id=1, source_target_pairs={{0,4},{1,5},{2,6},{3,7},{4,0},{5,1},{6,2},{7,3},{8,12},{9,13},{10,... | collective-permute-start | bytes 1376264 | tf_op jit(solution)/shard_map/ppermute | solution.py:29
  38.1 1.9 collective-permute-start.7
  40.5 14.3 %collective-permute-done.8 = f32[4,16,128]{2,1,0:T(8,128)S(1)} collective-permute-done((f32[4,16,128]{2,1,0:T(8,128)S(1)}, f32[4,16,128]{2,1,0:T(8,128)S(1)}, u32[]{:S(2)}, u32[]{:S(2)}) %collective-permute-start.8) | collective-permute-done | bytes 32800 | tf_op jit(solution)/shard_map/ppermute | solution.py:29
  57.5 2.8 %collective-permute-done.10 = f32[8,16,128]{2,1,0:T(8,128)S(1)} collective-permute-done((f32[8,16,128]{2,1,0:T(8,128)S(1)}, f32[8,16,128]{2,1,0:T(8,128)S(1)}, u32[]{:S(2)}, u32[]{:S(2)}) %collective-permute-start.10) | collective-permute-done | bytes 65568 | tf_op jit(solution)/shard_map/ppermute | solution.py:29
  62.5 4.1 %collective-permute-start.12 = (bf16[64,3584]{1,0:T(8,128)(2,1)S(1)}, bf16[64,3584]{1,0:T(8,128)(2,1)S(1)}, u32[]{:S(2)}, u32[]{:S(2)}) collective-permute-start(bf16[64,3584]{1,0:T(8,128)(2,1)S(1)} %pad_maximum_fusion.4), channel_id=1, source_target_pairs={{0,4},{1,5},{2,6},{3,7},{4,0},{5,1},{6,2},{7,3},{8,12},{9,13},{10,... | collective-permute-start | bytes 1376264 | tf_op jit(solution)/shard_map/ppermute | solution.py:29
  66.6 1.8 collective-permute-start.13
  68.3 12.1 %fusion.6 = f32[512,2048]{1,0:T(8,128)S(1)} fusion(bf16[3584,3072]{1,0:T(8,128)(2,1)} %bitcast.35, bf16[256,3584]{1,0:T(8,128)(2,1)} %collective-permute-done.9, bf16[256,3584]{1,0:T(8,128)(2,1)} %constant_dynamic-update-slice_fusion.10), kind=kOutput, calls=%fused_computation.6 | convolution fusion | flops 7523532800 | bytes 22544384 | tf_op jit(solution)/shard_map/dot_general | solution.py:34
  80.4 7.1 %multiply_convert_fusion.3 = bf16[512,3584]{1,0:T(8,128)(2,1)S(1)} fusion(bf16[3584,3072]{1,0:T(8,128)(2,1)} %bitcast.36, f32[512]{0:T(512)S(1)} %mul.71, f32[512,2048]{1,0:T(8,128)S(1)} %fusion.6), kind=kOutput, calls=%fused_computation.11 | convolution fusion | flops 3764912128 | bytes 15206400 | tf_op jit(solution)/shard_map/dot_general | solution.py:36
  88.7 3.0 %collective-permute-done.14 = bf16[256,3584]{1,0:T(8,128)(2,1)S(1)} collective-permute-done((bf16[256,3584]{1,0:T(8,128)(2,1)S(1)}, bf16[256,3584]{1,0:T(8,128)(2,1)S(1)}, u32[]{:S(2)}, u32[]{:S(2)}) %collective-permute-start.14) | collective-permute-done | bytes 1835040 | tf_op jit(solution)/shard_map/ppermute | solution.py:29
  91.7 2.6 collective-permute-done.15
  98.5 12.2 %fusion.4 = f32[512,2048]{1,0:T(8,128)S(1)} fusion(bf16[3584,3072]{1,0:T(8,128)(2,1)} %bitcast.37, bf16[256,3584]{1,0:T(8,128)(2,1)} %copy-done.5, bf16[256,3584]{1,0:T(8,128)(2,1)} %copy-done), kind=kOutput, calls=%fused_computation.4 | convolution fusion | flops 7523532800 | bytes 22544384 | tf_op jit(solution)/shard_map/dot_general | solution.py:34
  110.7 7.1 %multiply_convert_fusion.2 = bf16[512,3584]{1,0:T(8,128)(2,1)S(1)} fusion(bf16[3584,3072]{1,0:T(8,128)(2,1)} %bitcast.38, f32[512]{0:T(512)S(1)} %mul.76, f32[512,2048]{1,0:T(8,128)S(1)} %fusion.4), kind=kOutput, calls=%fused_computation.10 | convolution fusion | flops 3764912128 | bytes 15206400 | tf_op jit(solution)/shard_map/dot_general | solution.py:36
  117.8 10.2 %collective-permute-done.18 = bf16[64,3584]{1,0:T(8,128)(2,1)S(1)} collective-permute-done((bf16[64,3584]{1,0:T(8,128)(2,1)S(1)}, bf16[64,3584]{1,0:T(8,128)(2,1)S(1)}, u32[]{:S(2)}, u32[]{:S(2)}) %collective-permute-start.18) | collective-permute-done | bytes 458784 | tf_op jit(solution)/shard_map/ppermute | solution.py:29
  130.6 1.5 collective-permute-done.19
  132.1 2.6 collective-permute-done.20
  139.3 12.3 %fusion.2 = f32[512,2048]{1,0:T(8,128)S(1)} fusion(bf16[3584,3072]{1,0:T(8,128)(2,1)} %bitcast.39, bf16[256,3584]{1,0:T(8,128)(2,1)} %copy-done.4, bf16[256,3584]{1,0:T(8,128)(2,1)} %copy-done.1), kind=kOutput, calls=%fused_computation.2 | convolution fusion | flops 7523532800 | bytes 22544384 | tf_op jit(solution)/shard_map/dot_general | solution.py:34
  151.6 7.1 %multiply_convert_fusion.1 = bf16[512,3584]{1,0:T(8,128)(2,1)S(1)} fusion(bf16[3584,3072]{1,0:T(8,128)(2,1)} %bitcast.40, f32[512]{0:T(512)S(1)} %mul.81, f32[512,2048]{1,0:T(8,128)S(1)} %fusion.2), kind=kOutput, calls=%fused_computation.9 | convolution fusion | flops 3764912128 | bytes 15206400 | tf_op jit(solution)/shard_map/dot_general | solution.py:36
  159.5 9.1 %collective-permute-done.23 = bf16[128,3584]{1,0:T(8,128)(2,1)S(1)} collective-permute-done((bf16[128,3584]{1,0:T(8,128)(2,1)S(1)}, bf16[128,3584]{1,0:T(8,128)(2,1)S(1)}, u32[]{:S(2)}, u32[]{:S(2)}) %collective-permute-start.23) | collective-permute-done | bytes 917536 | tf_op jit(solution)/shard_map/ppermute | solution.py:29
  172.6 2.6 collective-permute-done.25
  179.1 1.6 collective-permute-start.28
  180.8 12.3 %fusion = f32[512,2048]{1,0:T(8,128)S(1)} fusion(bf16[3584,3072]{1,0:T(8,128)(2,1)} %bitcast.41, bf16[256,3584]{1,0:T(8,128)(2,1)} %copy-done.3, bf16[256,3584]{1,0:T(8,128)(2,1)} %copy-done.2), kind=kOutput, calls=%fused_computation | convolution fusion | flops 7523532800 | bytes 22544384 | tf_op jit(solution)/shard_map/dot_general | solution.py:34
  193.2 7.1 %multiply_convert_fusion = bf16[512,3584]{1,0:T(8,128)(2,1)S(1)} fusion(bf16[3584,3072]{1,0:T(8,128)(2,1)} %bitcast.42, f32[512]{0:T(512)S(1)} %mul.86, f32[512,2048]{1,0:T(8,128)S(1)} %fusion), kind=kOutput, calls=%fused_computation.8 | convolution fusion | flops 3764912128 | bytes 15206400 | tf_op jit(solution)/shard_map/dot_general | solution.py:36
  200.3 5.5 %collective-permute-done.28 = bf16[128,3584]{1,0:T(8,128)(2,1)S(1)} collective-permute-done((bf16[128,3584]{1,0:T(8,128)(2,1)S(1)}, bf16[128,3584]{1,0:T(8,128)(2,1)S(1)}, u32[]{:S(2)}, u32[]{:S(2)}) %collective-permute-start.28) | collective-permute-done | bytes 917536 | tf_op jit(solution)/shard_map/ppermute | solution.py:29
  211.9 2.4 collective-permute-start.30
  214.4 22.3 %collective-permute-done.30 = bf16[32,3584]{1,0:T(8,128)(2,1)S(1)} collective-permute-done((bf16[32,3584]{1,0:T(8,128)(2,1)S(1)}, bf16[32,3584]{1,0:T(8,128)(2,1)S(1)}, u32[]{:S(2)}, u32[]{:S(2)}) %collective-permute-start.30) | collective-permute-done | bytes 229408 | tf_op jit(solution)/shard_map/ppermute | solution.py:29
  236.7 2.2 collective-permute-done.32
  241.5 9.9 %collective-permute-done.33 = bf16[32,3584]{1,0:T(8,128)(2,1)S(1)} collective-permute-done((bf16[32,3584]{1,0:T(8,128)(2,1)S(1)}, bf16[32,3584]{1,0:T(8,128)(2,1)S(1)}, u32[]{:S(2)}, u32[]{:S(2)}) %collective-permute-start.33) | collective-permute-done | bytes 229408 | tf_op jit(solution)/shard_map/ppermute | solution.py:29
  253.8 10.0 %collective-permute-done.35 = bf16[32,3584]{1,0:T(8,128)(2,1)S(1)} collective-permute-done((bf16[32,3584]{1,0:T(8,128)(2,1)S(1)}, bf16[32,3584]{1,0:T(8,128)(2,1)S(1)}, u32[]{:S(2)}, u32[]{:S(2)}) %collective-permute-start.35) | collective-permute-done | bytes 229408 | tf_op jit(solution)/shard_map/ppermute | solution.py:29
  (134 shorter events, 44.5 us)
Async XLA Ops:
  1.3 15.0 %collective-permute-start = (bf16[32,3584]{1,0:T(8,128)(2,1)S(1)}, bf16[32,3584]{1,0:T(8,128)(2,1)S(1)}, u32[]{:S(2)}, u32[]{:S(2)}) collective-permute-start(bf16[32,3584]{1,0:T(8,128)(2,1)S(1)} %get-tuple-element.111), channel_id=1, source_target_pairs={{0,8},{1,9},{2,10},{3,11},{4,12},{5,13},{6,14},{7,15},{8,0},{9,1},... | collective-permute-start | bytes 688136 | tf_op jit(solution)/shard_map/ppermute | solution.py:29
  7.7 8.6 %collective-permute-start.1 = (f32[1,16,128]{2,1,0:T(8,128)S(1)}, f32[1,16,128]{2,1,0:T(8,128)S(1)}, u32[]{:S(2)}, u32[]{:S(2)}) collective-permute-start(f32[1,16,128]{2,1,0:T(8,128)S(1)} %fusion.41), channel_id=1, source_target_pairs={{0,8},{1,9},{2,10},{3,11},{4,12},{5,13},{6,14},{7,15},{8,0},{9,1},... | collective-permute-start | bytes 24584 | tf_op jit(solution)/shard_map/ppermute | solution.py:29
  16.4 17.0 %collective-permute-start.2 = (bf16[64,3584]{1,0:T(8,128)(2,1)S(1)}, bf16[64,3584]{1,0:T(8,128)(2,1)S(1)}, u32[]{:S(2)}, u32[]{:S(2)}) collective-permute-start(bf16[64,3584]{1,0:T(8,128)(2,1)S(1)} %constant_dynamic-update-slice_fusion), channel_id=1, source_target_pairs={{0,4},{1,5},{2,6},{3,7},{4,0},{5,1},{6,2},{7,3},{8,12},{9,13},{10,... | collective-permute-start | bytes 1376264 | tf_op jit(solution)/shard_map/ppermute | solution.py:29
  17.1 16.3 %collective-permute-start.3 = (bf16[32,3584]{1,0:T(8,128)(2,1)S(1)}, bf16[32,3584]{1,0:T(8,128)(2,1)S(1)}, u32[]{:S(2)}, u32[]{:S(2)}) collective-permute-start(bf16[32,3584]{1,0:T(8,128)(2,1)S(1)} %get-tuple-element.120), channel_id=1, source_target_pairs={{0,8},{1,9},{2,10},{3,11},{4,12},{5,13},{6,14},{7,15},{8,0},{9,1},... | collective-permute-start | bytes 688136 | tf_op jit(solution)/shard_map/ppermute | solution.py:29
  20.5 12.9 %collective-permute-start.4 = (f32[2,16,128]{2,1,0:T(8,128)S(1)}, f32[2,16,128]{2,1,0:T(8,128)S(1)}, u32[]{:S(2)}, u32[]{:S(2)}) collective-permute-start(f32[2,16,128]{2,1,0:T(8,128)S(1)} %constant_dynamic-update-slice_fusion.2), channel_id=1, source_target_pairs={{0,4},{1,5},{2,6},{3,7},{4,0},{5,1},{6,2},{7,3},{8,12},{9,13},{10,... | collective-permute-start | bytes 49160 | tf_op jit(solution)/shard_map/ppermute | solution.py:29
  33.5 21.4 %collective-permute-start.5 = (bf16[128,3584]{1,0:T(8,128)(2,1)S(1)}, bf16[128,3584]{1,0:T(8,128)(2,1)S(1)}, u32[]{:S(2)}, u32[]{:S(2)}) collective-permute-start(bf16[128,3584]{1,0:T(8,128)(2,1)S(1)} %constant_dynamic-update-slice_fusion.4), channel_id=1, source_target_pairs={{0,2},{1,3},{2,0},{3,1},{4,6},{5,7},{6,4},{7,5},{8,10},{9,11},{10,... | collective-permute-start | bytes 2752520 | tf_op jit(solution)/shard_map/ppermute | solution.py:29
  34.9 20.0 %collective-permute-start.6 = (bf16[64,3584]{1,0:T(8,128)(2,1)S(1)}, bf16[64,3584]{1,0:T(8,128)(2,1)S(1)}, u32[]{:S(2)}, u32[]{:S(2)}) collective-permute-start(bf16[64,3584]{1,0:T(8,128)(2,1)S(1)} %constant_dynamic-update-slice_fusion.6), channel_id=1, source_target_pairs={{0,4},{1,5},{2,6},{3,7},{4,0},{5,1},{6,2},{7,3},{8,12},{9,13},{10,... | collective-permute-start | bytes 1376264 | tf_op jit(solution)/shard_map/ppermute | solution.py:29
  38.1 16.8 %collective-permute-start.7 = (bf16[32,3584]{1,0:T(8,128)(2,1)S(1)}, bf16[32,3584]{1,0:T(8,128)(2,1)S(1)}, u32[]{:S(2)}, u32[]{:S(2)}) collective-permute-start(bf16[32,3584]{1,0:T(8,128)(2,1)S(1)} %get-tuple-element.130), channel_id=1, source_target_pairs={{0,8},{1,9},{2,10},{3,11},{4,12},{5,13},{6,14},{7,15},{8,0},{9,1},... | collective-permute-start | bytes 688136 | tf_op jit(solution)/shard_map/ppermute | solution.py:29
  40.0 14.8 %collective-permute-start.8 = (f32[4,16,128]{2,1,0:T(8,128)S(1)}, f32[4,16,128]{2,1,0:T(8,128)S(1)}, u32[]{:S(2)}, u32[]{:S(2)}) collective-permute-start(f32[4,16,128]{2,1,0:T(8,128)S(1)} %constant_dynamic-update-slice_fusion.8), channel_id=1, source_target_pairs={{0,2},{1,3},{2,0},{3,1},{4,6},{5,7},{6,4},{7,5},{8,10},{9,11},{10,... | collective-permute-start | bytes 98312 | tf_op jit(solution)/shard_map/ppermute | solution.py:29
  56.9 4.2 %collective-permute-start.9 = (bf16[256,3584]{1,0:T(8,128)(2,1)}, bf16[256,3584]{1,0:T(8,128)(2,1)}, u32[]{:S(2)}, u32[]{:S(2)}) collective-permute-start(bf16[256,3584]{1,0:T(8,128)(2,1)} %constant_dynamic-update-slice_fusion.10), channel_id=1, source_target_pairs={{0,1},{1,0},{2,3},{3,2},{4,5},{5,4},{6,7},{7,6},{8,9},{9,8},{10,11... | collective-permute-start | bytes 5505032 | tf_op jit(solution)/shard_map/ppermute | solution.py:29
  61.2 26.4 %collective-permute-start.11 = (bf16[128,3584]{1,0:T(8,128)(2,1)S(1)}, bf16[128,3584]{1,0:T(8,128)(2,1)S(1)}, u32[]{:S(2)}, u32[]{:S(2)}) collective-permute-start(bf16[128,3584]{1,0:T(8,128)(2,1)S(1)} %pad_maximum_fusion), channel_id=1, source_target_pairs={{0,2},{1,3},{2,0},{3,1},{4,6},{5,7},{6,4},{7,5},{8,10},{9,11},{10,... | collective-permute-start | bytes 2752520 | tf_op jit(solution)/shard_map/ppermute | solution.py:29
  62.5 25.1 %collective-permute-start.12 = (bf16[64,3584]{1,0:T(8,128)(2,1)S(1)}, bf16[64,3584]{1,0:T(8,128)(2,1)S(1)}, u32[]{:S(2)}, u32[]{:S(2)}) collective-permute-start(bf16[64,3584]{1,0:T(8,128)(2,1)S(1)} %pad_maximum_fusion.4), channel_id=1, source_target_pairs={{0,4},{1,5},{2,6},{3,7},{4,0},{5,1},{6,2},{7,3},{8,12},{9,13},{10,... | collective-permute-start | bytes 1376264 | tf_op jit(solution)/shard_map/ppermute | solution.py:29
  66.6 21.0 %collective-permute-start.13 = (bf16[32,3584]{1,0:T(8,128)(2,1)S(1)}, bf16[32,3584]{1,0:T(8,128)(2,1)S(1)}, u32[]{:S(2)}, u32[]{:S(2)}) collective-permute-start(bf16[32,3584]{1,0:T(8,128)(2,1)S(1)} %get-tuple-element.147), channel_id=1, source_target_pairs={{0,8},{1,9},{2,10},{3,11},{4,12},{5,13},{6,14},{7,15},{8,0},{9,1},... | collective-permute-start | bytes 688136 | tf_op jit(solution)/shard_map/ppermute | solution.py:29
  87.8 3.9 %collective-permute-start.14 = (bf16[256,3584]{1,0:T(8,128)(2,1)S(1)}, bf16[256,3584]{1,0:T(8,128)(2,1)S(1)}, u32[]{:S(2)}, u32[]{:S(2)}) collective-permute-start(bf16[256,3584]{1,0:T(8,128)(2,1)S(1)} %get-tuple-element.225), channel_id=1, source_target_pairs={{0,1},{1,0},{2,3},{3,2},{4,5},{5,4},{6,7},{7,6},{8,9},{9,8},{10,11... | collective-permute-start | bytes 5505032 | tf_op jit(solution)/shard_map/ppermute | solution.py:29
  88.1 6.2 %collective-permute-start.15 = (bf16[256,3584]{1,0:T(8,128)(2,1)S(1)}, bf16[256,3584]{1,0:T(8,128)(2,1)S(1)}, u32[]{:S(2)}, u32[]{:S(2)}) collective-permute-start(bf16[256,3584]{1,0:T(8,128)(2,1)S(1)} %constant_dynamic-update-slice_fusion.14), channel_id=1, source_target_pairs={{0,1},{1,0},{2,3},{3,2},{4,5},{5,4},{6,7},{7,6},{8,9},{9,8},{10,11... | collective-permute-start | bytes 5505032 | tf_op jit(solution)/shard_map/ppermute | solution.py:29
  95.7 32.3 %collective-permute-start.16 = (bf16[128,3584]{1,0:T(8,128)(2,1)S(1)}, bf16[128,3584]{1,0:T(8,128)(2,1)}, u32[]{:S(2)}, u32[]{:S(2)}) collective-permute-start(bf16[128,3584]{1,0:T(8,128)(2,1)S(1)} %bitcast.27), channel_id=1, source_target_pairs={{0,4},{1,5},{2,6},{3,7},{4,0},{5,1},{6,2},{7,3},{8,12},{9,13},{10,... | collective-permute-start | bytes 2752520 | tf_op jit(solution)/shard_map/ppermute | solution.py:29
  96.2 31.8 %collective-permute-start.17 = (bf16[128,3584]{1,0:T(8,128)(2,1)S(1)}, bf16[128,3584]{1,0:T(8,128)(2,1)S(1)}, u32[]{:S(2)}, u32[]{:S(2)}) collective-permute-start(bf16[128,3584]{1,0:T(8,128)(2,1)S(1)} %pad_maximum_fusion.1), channel_id=1, source_target_pairs={{0,2},{1,3},{2,0},{3,1},{4,6},{5,7},{6,4},{7,5},{8,10},{9,11},{10,... | collective-permute-start | bytes 2752520 | tf_op jit(solution)/shard_map/ppermute | solution.py:29
  97.3 30.7 %collective-permute-start.18 = (bf16[64,3584]{1,0:T(8,128)(2,1)S(1)}, bf16[64,3584]{1,0:T(8,128)(2,1)S(1)}, u32[]{:S(2)}, u32[]{:S(2)}) collective-permute-start(bf16[64,3584]{1,0:T(8,128)(2,1)S(1)} %pad_maximum_fusion.5), channel_id=1, source_target_pairs={{0,4},{1,5},{2,6},{3,7},{4,0},{5,1},{6,2},{7,3},{8,12},{9,13},{10,... | collective-permute-start | bytes 1376264 | tf_op jit(solution)/shard_map/ppermute | solution.py:29
  128.5 6.2 %collective-permute-start.20 = (bf16[256,3584]{1,0:T(8,128)(2,1)S(1)}, bf16[256,3584]{1,0:T(8,128)(2,1)S(1)}, u32[]{:S(2)}, u32[]{:S(2)}) collective-permute-start(bf16[256,3584]{1,0:T(8,128)(2,1)S(1)} %constant_dynamic-update-slice_fusion.16), channel_id=1, source_target_pairs={{0,1},{1,0},{2,3},{3,2},{4,5},{5,4},{6,7},{7,6},{8,9},{9,8},{10,11... | collective-permute-start | bytes 5505032 | tf_op jit(solution)/shard_map/ppermute | solution.py:29
  136.1 22.6 %collective-permute-start.21 = (bf16[64,3584]{1,0:T(8,128)(2,1)}, bf16[64,3584]{1,0:T(8,128)(2,1)}, u32[]{:S(2)}, u32[]{:S(2)}) collective-permute-start(bf16[64,3584]{1,0:T(8,128)(2,1)} %get-tuple-element.241), channel_id=1, source_target_pairs={{0,2},{1,3},{2,0},{3,1},{4,6},{5,7},{6,4},{7,5},{8,10},{9,11},{10,... | collective-permute-start | bytes 1376264 | tf_op jit(solution)/shard_map/ppermute | solution.py:29
  137.2 22.3 %collective-permute-start.22 = (bf16[128,3584]{1,0:T(8,128)(2,1)S(1)}, bf16[128,3584]{1,0:T(8,128)(2,1)}, u32[]{:S(2)}, u32[]{:S(2)}) collective-permute-start(bf16[128,3584]{1,0:T(8,128)(2,1)S(1)} %bitcast.29), channel_id=1, source_target_pairs={{0,4},{1,5},{2,6},{3,7},{4,0},{5,1},{6,2},{7,3},{8,12},{9,13},{10,... | collective-permute-start | bytes 2752520 | tf_op jit(solution)/shard_map/ppermute | solution.py:29
  138.3 30.3 %collective-permute-start.23 = (bf16[128,3584]{1,0:T(8,128)(2,1)S(1)}, bf16[128,3584]{1,0:T(8,128)(2,1)S(1)}, u32[]{:S(2)}, u32[]{:S(2)}) collective-permute-start(bf16[128,3584]{1,0:T(8,128)(2,1)S(1)} %pad_maximum_fusion.2), channel_id=1, source_target_pairs={{0,2},{1,3},{2,0},{3,1},{4,6},{5,7},{6,4},{7,5},{8,10},{9,11},{10,... | collective-permute-start | bytes 2752520 | tf_op jit(solution)/shard_map/ppermute | solution.py:29
  169.0 6.2 %collective-permute-start.25 = (bf16[256,3584]{1,0:T(8,128)(2,1)S(1)}, bf16[256,3584]{1,0:T(8,128)(2,1)S(1)}, u32[]{:S(2)}, u32[]{:S(2)}) collective-permute-start(bf16[256,3584]{1,0:T(8,128)(2,1)S(1)} %constant_dynamic-update-slice_fusion.18), channel_id=1, source_target_pairs={{0,1},{1,0},{2,3},{3,2},{4,5},{5,4},{6,7},{7,6},{8,9},{9,8},{10,11... | collective-permute-start | bytes 5505032 | tf_op jit(solution)/shard_map/ppermute | solution.py:29
  176.0 24.2 %collective-permute-start.26 = (bf16[32,3584]{1,0:T(8,128)(2,1)}, bf16[32,3584]{1,0:T(8,128)(2,1)}, u32[]{:S(2)}, u32[]{:S(2)}) collective-permute-start(bf16[32,3584]{1,0:T(8,128)(2,1)} %get-tuple-element.253), channel_id=1, source_target_pairs={{0,8},{1,9},{2,10},{3,11},{4,12},{5,13},{6,14},{7,15},{8,0},{9,1},... | collective-permute-start | bytes 688136 | tf_op jit(solution)/shard_map/ppermute | solution.py:29
  178.0 22.3 %collective-permute-start.27 = (bf16[64,3584]{1,0:T(8,128)(2,1)}, bf16[64,3584]{1,0:T(8,128)(2,1)}, u32[]{:S(2)}, u32[]{:S(2)}) collective-permute-start(bf16[64,3584]{1,0:T(8,128)(2,1)} %get-tuple-element.239), channel_id=1, source_target_pairs={{0,2},{1,3},{2,0},{3,1},{4,6},{5,7},{6,4},{7,5},{8,10},{9,11},{10,... | collective-permute-start | bytes 1376264 | tf_op jit(solution)/shard_map/ppermute | solution.py:29
  179.1 26.7 %collective-permute-start.28 = (bf16[128,3584]{1,0:T(8,128)(2,1)S(1)}, bf16[128,3584]{1,0:T(8,128)(2,1)S(1)}, u32[]{:S(2)}, u32[]{:S(2)}) collective-permute-start(bf16[128,3584]{1,0:T(8,128)(2,1)S(1)} %bitcast.28), channel_id=1, source_target_pairs={{0,4},{1,5},{2,6},{3,7},{4,0},{5,1},{6,2},{7,3},{8,12},{9,13},{10,... | collective-permute-start | bytes 2752520 | tf_op jit(solution)/shard_map/ppermute | solution.py:29
  210.0 26.8 %collective-permute-start.31 = (bf16[64,3584]{1,0:T(8,128)(2,1)S(1)}, bf16[64,3584]{1,0:T(8,128)(2,1)S(1)}, u32[]{:S(2)}, u32[]{:S(2)}) collective-permute-start(bf16[64,3584]{1,0:T(8,128)(2,1)S(1)} %get-tuple-element.237), channel_id=1, source_target_pairs={{0,2},{1,3},{2,0},{3,1},{4,6},{5,7},{6,4},{7,5},{8,10},{9,11},{10,... | collective-permute-start | bytes 1376264 | tf_op jit(solution)/shard_map/ppermute | solution.py:29
  211.8 27.1 %collective-permute-start.32 = (bf16[128,3584]{1,0:T(8,128)(2,1)S(1)}, bf16[128,3584]{1,0:T(8,128)(2,1)S(1)}, u32[]{:S(2)}, u32[]{:S(2)}) collective-permute-start(bf16[128,3584]{1,0:T(8,128)(2,1)S(1)} %bitcast.30), channel_id=1, source_target_pairs={{0,4},{1,5},{2,6},{3,7},{4,0},{5,1},{6,2},{7,3},{8,12},{9,13},{10,... | collective-permute-start | bytes 2752520 | tf_op jit(solution)/shard_map/ppermute | solution.py:29
  211.9 24.8 %collective-permute-start.30 = (bf16[32,3584]{1,0:T(8,128)(2,1)S(1)}, bf16[32,3584]{1,0:T(8,128)(2,1)S(1)}, u32[]{:S(2)}, u32[]{:S(2)}) collective-permute-start(bf16[32,3584]{1,0:T(8,128)(2,1)S(1)} %get-tuple-element.251), channel_id=1, source_target_pairs={{0,8},{1,9},{2,10},{3,11},{4,12},{5,13},{6,14},{7,15},{8,0},{9,1},... | collective-permute-start | bytes 688136 | tf_op jit(solution)/shard_map/ppermute | solution.py:29
  239.1 12.4 %collective-permute-start.33 = (bf16[32,3584]{1,0:T(8,128)(2,1)S(1)}, bf16[32,3584]{1,0:T(8,128)(2,1)S(1)}, u32[]{:S(2)}, u32[]{:S(2)}) collective-permute-start(bf16[32,3584]{1,0:T(8,128)(2,1)S(1)} %get-tuple-element.249), channel_id=1, source_target_pairs={{0,8},{1,9},{2,10},{3,11},{4,12},{5,13},{6,14},{7,15},{8,0},{9,1},... | collective-permute-start | bytes 688136 | tf_op jit(solution)/shard_map/ppermute | solution.py:29
  240.6 11.5 %collective-permute-start.34 = (bf16[64,3584]{1,0:T(8,128)(2,1)S(1)}, bf16[64,3584]{1,0:T(8,128)(2,1)S(1)}, u32[]{:S(2)}, u32[]{:S(2)}) collective-permute-start(bf16[64,3584]{1,0:T(8,128)(2,1)S(1)} %get-tuple-element.235), channel_id=1, source_target_pairs={{0,2},{1,3},{2,0},{3,1},{4,6},{5,7},{6,4},{7,5},{8,10},{9,11},{10,... | collective-permute-start | bytes 1376264 | tf_op jit(solution)/shard_map/ppermute | solution.py:29
  252.3 11.5 %collective-permute-start.35 = (bf16[32,3584]{1,0:T(8,128)(2,1)S(1)}, bf16[32,3584]{1,0:T(8,128)(2,1)S(1)}, u32[]{:S(2)}, u32[]{:S(2)}) collective-permute-start(bf16[32,3584]{1,0:T(8,128)(2,1)S(1)} %get-tuple-element.247), channel_id=1, source_target_pairs={{0,8},{1,9},{2,10},{3,11},{4,12},{5,13},{6,14},{7,15},{8,0},{9,1},... | collective-permute-start | bytes 688136 | tf_op jit(solution)/shard_map/ppermute | solution.py:29
  (10 other events, 36.3 us)
